TPU v7x, 512 devices: a whole 4x4x16 slice. The times are simulated.
512 devices in a mesh: img: 64 (over y, z), blk: 8 (over x, core).
Axes of the slice: x: 4, y: 4, z: 16, core: 2. Of those that a mesh axis runs over, the one named last changes fastest.
Arguments:
- descriptors: bfloat16 [1024, 128, 256], P(('img', 'blk')), may hold values from -8 to 8
- covisible: int32 [1024, 6], P(('img', 'blk')), may hold values from 0 to 1023, as said below
- tile_counts: int32 [1024], P(('img', 'blk')), may hold values from 1 to 6, as said below
- keypoints: int32 [1024], replicated, may hold values from 32 to 128, as said below
- query_weight: bfloat16 [256, 256], replicated, may hold values from -0.375 to 0.375
- key_weight: bfloat16 [256, 256], replicated, may hold values from -0.375 to 0.375
- value_weight: bfloat16 [256, 256], replicated, may hold values from -0.375 to 0.375
- merge_weight: bfloat16 [512, 512], replicated, may hold values from -0.25 to 0.25
- output_weight: bfloat16 [512, 256], replicated, may hold values from -0.25 to 0.25
- dustbin: float32 [1], replicated, may hold values from 0.5 to 2
Outputs:
- plan: float32 [1024, 6, 128, 128], P(('img', 'blk'))
- row_bin: float32 [1024, 128], P(('img', 'blk'))
- col_bin: float32 [1024, 128], P(('img', 'blk'))
Inputs may be any that keep to these rules, and one draw needn't show every extreme that they name: `covisible`: the 6 entries of a block's row name different blocks, never the block itself, all within its own image group of 16 consecutive blocks or the groups just before and after it. `tile_counts`: some block uses all 6 of its listed blocks. The valid keypoints of a block are its first ones; some block is full.
All inputs are finite; a program needn't handle non-finite values.
Results may differ from a plain program's by a relative error of at most 0.0032.
Values may be sent and summed in bfloat16 or wider, within the bound.
No kernel may reach another device: no remote copies, remote signals or barrier semaphores. Data moves between devices by JAX's collectives and lax.ppermute only.
A program may use at most 64 MiB of HBM per device.

v0:
```python
import math

import jax
import jax.numpy as jnp
from jax import lax
from jax.sharding import PartitionSpec as P

HEADS = 4
ITERS = 3


def copy_for_each(array, axis):
    copies = jnp.broadcast_to(array, (lax.axis_size(axis), *array.shape))
    return lax.all_to_all(copies, axis, split_axis=0, concat_axis=0, tiled=True)


def in_order(blocks, dim):
    blocks = jnp.moveaxis(blocks, 0, dim)
    lengths = blocks.shape
    return blocks.reshape(*lengths[:dim], lengths[dim] * lengths[dim + 1], *lengths[dim + 2 :])


def gather_directly(array, axis, dim):
    blocks = copy_for_each(array, axis)
    return in_order(blocks, dim)


def with_halo(block, sides, width):
    for axis, dim in sides:
        count = lax.axis_size(axis)
        forward = [(i, i + 1) for i in range(count - 1)]
        backward = [(target, source) for source, target in forward]
        low = lax.ppermute(
            lax.slice_in_dim(block, block.shape[dim] - width, None, axis=dim), axis, forward
        )
        high = lax.ppermute(lax.slice_in_dim(block, 0, width, axis=dim), axis, backward)
        block = jnp.concatenate([low, block, high], axis=dim)
    return block


def split_up(array, dim, size):
    lengths = array.shape
    blocks = array.reshape(*lengths[:dim], size, lengths[dim] // size, *lengths[dim + 1 :])
    return jnp.moveaxis(blocks, dim, 0)


def summed_on_arrival(array, axis, dim):
    blocks = split_up(array, dim, lax.axis_size(axis))
    arrived = lax.all_to_all(blocks, axis, split_axis=0, concat_axis=0, tiled=True)
    return arrived.sum(axis=0)


def shifted_2(block, axis, distance):
    devices = range(lax.axis_size(axis))
    route = [(i - distance, i) for i in devices if i - distance in devices]
    return lax.ppermute(block, axis, route)


def project_rows(values, weight):
    flat = jnp.dot(values.reshape(-1, values.shape[-1]), weight, preferred_element_type=jnp.float32)
    return flat.reshape(values.shape[:-1] + (weight.shape[1],)).astype(jnp.bfloat16)


def on_device(
    descriptors,
    covisible,
    tile_counts,
    keypoints,
    query_weight,
    key_weight,
    value_weight,
    merge_weight,
    output_weight,
    dustbin,
):
    local_blocks, block_len, feature_dim = descriptors.shape
    head_dim = feature_dim // HEADS
    tile_count = covisible.shape[1]
    blk_count = lax.axis_size("blk")
    group_size = local_blocks * blk_count
    near_count = 3 * group_size
    group_index = lax.axis_index("img")
    blk_index = lax.axis_index("blk")
    first_block = (group_index - 1) * group_size
    near_ids = covisible - first_block
    padding = jnp.zeros((group_size,), jnp.int32)
    padded_counts = jnp.concatenate([padding, keypoints, padding])
    near_kpts = lax.dynamic_slice_in_dim(padded_counts, group_index * group_size, near_count)
    own_kpts = lax.dynamic_slice_in_dim(
        keypoints, (group_index * blk_count + blk_index) * local_blocks, local_blocks
    )
    slot_hit = near_ids[:, :, None] == jnp.arange(near_count, dtype=jnp.int32)[None, None, :]
    tile_kpts = jnp.sum(jnp.where(slot_hit, near_kpts[None, None, :], 0), axis=2)
    positions = jnp.arange(block_len, dtype=jnp.int32)
    tile_live = jnp.arange(tile_count, dtype=jnp.int32)[None, :] < tile_counts[:, None]
    key_live = tile_live[:, :, None] & (positions[None, None, :] < tile_kpts[:, :, None])
    row_live = positions[None, :] < own_kpts[:, None]
    query = project_rows(descriptors, query_weight)
    group_desc = gather_directly(descriptors, "blk", 0)
    near_desc = with_halo(group_desc, (("img", 0),), group_size)
    near_keys = project_rows(near_desc, key_weight)
    near_values = project_rows(near_desc, value_weight)
    key_tiles = jnp.take(near_keys, near_ids, axis=0).reshape(
        local_blocks, tile_count * block_len, HEADS, head_dim
    )
    value_tiles = jnp.take(near_values, near_ids, axis=0).reshape(
        local_blocks, tile_count * block_len, HEADS, head_dim
    )
    logits = jnp.einsum(
        "rqhd,rkhd->rhqk",
        query.reshape(local_blocks, block_len, HEADS, head_dim),
        key_tiles,
        preferred_element_type=jnp.float32,
    ) / math.sqrt(head_dim)
    logits = jnp.where(key_live.reshape(local_blocks, 1, 1, tile_count * block_len), logits, -1e30)
    highest = jnp.max(logits, axis=3, keepdims=True)
    weights = jnp.exp(logits - highest)
    weights = (weights / jnp.sum(weights, axis=3, keepdims=True)).astype(jnp.bfloat16)
    message = jnp.einsum(
        "rhqk,rkhd->rqhd", weights, value_tiles, preferred_element_type=jnp.float32
    )
    message = message.reshape(local_blocks, block_len, feature_dim).astype(jnp.bfloat16)
    joined = jnp.concatenate([descriptors, message], axis=2).reshape(-1, 2 * feature_dim)
    hidden = jnp.maximum(
        jnp.dot(joined, merge_weight, preferred_element_type=jnp.float32), 0.0
    ).astype(jnp.bfloat16)
    refined = descriptors.reshape(-1, feature_dim).astype(jnp.float32) + jnp.dot(
        hidden, output_weight, preferred_element_type=jnp.float32
    )
    refined = refined.astype(jnp.bfloat16).reshape(local_blocks, block_len, feature_dim)
    group_refined = gather_directly(refined, "blk", 0)
    near_refined = with_halo(group_refined, (("img", 0),), group_size)
    match_tiles = jnp.take(near_refined, near_ids, axis=0)
    scores = jnp.einsum(
        "rid,rkjd->rkij", refined, match_tiles, preferred_element_type=jnp.float32
    ) / math.sqrt(feature_dim)
    valid = tile_live[:, :, None, None] & row_live[:, None, :, None] & key_live[:, :, None, :]
    dust = dustbin[0]
    own_pot = jnp.zeros((local_blocks, block_len), jnp.float32)
    near_pot = jnp.zeros((near_count, block_len), jnp.float32)
    row_pot = jnp.zeros((local_blocks, block_len), jnp.float32)
    placing = slot_hit.reshape(local_blocks * tile_count, near_count).astype(jnp.float32)
    for sweep in range(ITERS):
        tile_pot = jnp.take(near_pot, near_ids, axis=0)
        shifted = jnp.where(valid, scores + tile_pot[:, :, None, :], -1e30)
        highest_row = jnp.maximum(jnp.max(shifted, axis=(1, 3)), dust)
        total = jnp.sum(jnp.exp(shifted - highest_row[:, None, :, None]), axis=(1, 3)) + jnp.exp(
            dust - highest_row
        )
        row_pot = -(highest_row + jnp.log(total))
        mass = jnp.sum(
            jnp.where(
                valid, jnp.exp(scores + row_pot[:, None, :, None] + tile_pot[:, :, None, :]), 0.0
            ),
            axis=2,
        )
        spread = jnp.dot(placing.T, mass.reshape(-1, block_len), precision=lax.Precision.HIGHEST)
        sections = spread.reshape(3, blk_count, local_blocks, block_len)
        shares = summed_on_arrival(sections, "blk", 1)[:, 0]
        from_after = shifted_2(shares[0], "img", -1)
        from_before = shifted_2(shares[2], "img", 1)
        col_sum = shares[1] + from_after + from_before
        own_pot = own_pot - jnp.log(col_sum + jnp.exp(dust + own_pot))
        group_pot = gather_directly(own_pot, "blk", 0)
        near_pot = with_halo(group_pot, (("img", 0),), group_size)
    tile_pot = jnp.take(near_pot, near_ids, axis=0)
    plan = jnp.where(valid, scores + row_pot[:, None, :, None] + tile_pot[:, :, None, :], 0.0)
    row_bin = jnp.where(row_live, dust + row_pot, 0.0)
    col_bin = jnp.where(row_live, dust + own_pot, 0.0)
    return (plan, row_bin, col_bin)


def solution(mesh):
    in_specs = (
        P(("img", "blk"), None, None),
        P(("img", "blk"), None),
        P(("img", "blk")),
        P(),
        P(),
        P(),
        P(),
        P(),
        P(),
        P(),
    )
    out_specs = (
        P(("img", "blk"), None, None, None),
        P(("img", "blk"), None),
        P(("img", "blk"), None),
    )
    return jax.shard_map(
        on_device, mesh=mesh, in_specs=in_specs, out_specs=out_specs, check_vma=False
    )
```

profile of v0, /device:TPU:24, one launch (start us, length us, event | category | flops | bytes accessed | tf_op | source)
XLA Modules:
  0.0 259.8 jit_solution(5661582540391724014)
XLA Ops:
  0.7 2.1 broadcast_in_dim.109
  2.8 4.3 %all-to-all-start = ((bf16[8,2,128,256]{3,2,1,0:T(8,128)(2,1)}), bf16[8,2,128,256]{3,2,1,0:T(8,128)(2,1)S(1)}, u32[]{:S(2)}, u32[]{:S(2)}) async-start(bf16[8,2,128,256]{3,2,1,0:T(8,128)(2,1)} %broadcast_in_dim.109), calls=%async_computation | async-start | bytes 2097152 | tf_op jit(solution)/shard_map/all_to_all | solution.py:14
  7.9 15.1 %all-to-all-done = bf16[8,2,128,256]{3,2,1,0:T(8,128)(2,1)S(1)} async-done(((bf16[8,2,128,256]{3,2,1,0:T(8,128)(2,1)}), bf16[8,2,128,256]{3,2,1,0:T(8,128)(2,1)S(1)}, u32[]{:S(2)}, u32[]{:S(2)}) %all-to-all-start) | async-done | bytes 1048608 | tf_op jit(solution)/shard_map/all_to_all | solution.py:14
  23.1 11.6 %collective-permute-start.1 = (bf16[16,128,256]{2,1,0:T(8,128)(2,1)S(1)}, bf16[16,128,256]{2,1,0:T(8,128)(2,1)S(1)}, u32[]{:S(2)}, u32[]{:S(2)}) collective-permute-start(bf16[16,128,256]{2,1,0:T(8,128)(2,1)S(1)} %bitcast.165), channel_id=1, source_target_pairs={{8,0},{16,8},{24,16},{32,24},{40,32},{48,40},{56,48},{64,56},{72,6... | collective-permute-start | bytes 3145736 | tf_op jit(solution)/shard_map/ppermute | solution.py:36
  34.7 1.9 collective-permute-start
  38.5 18.4 %collective-permute-done.1 = bf16[16,128,256]{2,1,0:T(8,128)(2,1)S(1)} collective-permute-done((bf16[16,128,256]{2,1,0:T(8,128)(2,1)S(1)}, bf16[16,128,256]{2,1,0:T(8,128)(2,1)S(1)}, u32[]{:S(2)}, u32[]{:S(2)}) %collective-permute-start.1) | collective-permute-done | bytes 1048608 | tf_op jit(solution)/shard_map/ppermute | solution.py:36
  56.9 6.3 %collective-permute-done = bf16[16,128,256]{2,1,0:T(8,128)(2,1)} collective-permute-done((bf16[16,128,256]{2,1,0:T(8,128)(2,1)S(1)}, bf16[16,128,256]{2,1,0:T(8,128)(2,1)}, u32[]{:S(2)}, u32[]{:S(2)}) %collective-permute-start) | collective-permute-done | bytes 1048608 | tf_op jit(solution)/shard_map/ppermute | solution.py:33
  63.2 3.9 %convolution_convert_fusion = bf16[48,128,256]{2,1,0:T(8,128)(2,1)} fusion(bf16[16,128,256]{2,1,0:T(8,128)(2,1)S(1)} %collective-permute-done.1, bf16[16,128,256]{2,1,0:T(8,128)(2,1)S(1)} %bitcast.167, bf16[16,128,256]{2,1,0:T(8,128)(2,1)} %collective-permute-done, bf16[256,256]{1,0:T(8,128)(2,1)S(1)} %copy-done.12), kind=kOutput, calls=%fused_computation.14 | convolution fusion | flops 810024960 | bytes 6422528 | tf_op jit(solution)/shard_map/dot_general | solution.py:60
  67.1 2.5 gather_fusion.1
  69.6 3.9 %convolution_convert_fusion.1 = bf16[48,128,256]{2,1,0:T(8,128)(2,1)} fusion(bf16[16,128,256]{2,1,0:T(8,128)(2,1)S(1)} %collective-permute-done.1, bf16[16,128,256]{2,1,0:T(8,128)(2,1)S(1)} %bitcast.168, bf16[16,128,256]{2,1,0:T(8,128)(2,1)} %collective-permute-done, bf16[256,256]{1,0:T(8,128)(2,1)} %param.20), kind=kOutput, calls=%fused_computation.15 | convolution fusion | flops 810024960 | bytes 6422528 | tf_op jit(solution)/shard_map/dot_general | solution.py:60
  73.4 2.5 gather_fusion
  77.5 1.7 broadcast_select_fusion
  79.2 2.0 reshape.291
  81.2 2.0 reshape.289
  83.3 2.8 %fusion.62 = (f32[2,4,128]{2,1,0:T(4,128)S(1)}, f32[2,4,128,768]{3,2,1,0:T(8,128)}) fusion(pred[2,768]{1,0:T(4,128)(4,1)S(1)} %copy-done.7, bf16[2,128,4,64]{1,3,2,0:T(8,128)(2,1)S(1)} %bitcast.173, bf16[2,768,4,64]{1,3,2,0:T(8,128)(2,1)S(1)} %reshape.291), kind=kOutput, calls=%fused_computation.131 | convolution fusion | flops 103809792 | bytes 4068864 | tf_op jit(solution)/shard_map/sub | solution.py:117
  86.1 2.7 %fusion.10 = bf16[2,4,64,128]{3,2,1,0:T(8,128)(2,1)S(1)} fusion(bf16[2,768,4,64]{1,3,2,0:T(8,128)(2,1)S(1)} %reshape.289, f32[2,4,128,768]{3,2,1,0:T(8,128)} %get-tuple-element.35, f32[2,4,128]{2,1,0:T(4,128)S(1)} %get-tuple-element.34), kind=kOutput, calls=%fused_computation.34 | convolution fusion | flops 102301696 | bytes 4067328 | tf_op jit(solution)/shard_map/rhqk,rkhd->rqhd/dot_general | solution.py:119
  89.6 18.5 %all_to_all.40 = bf16[8,2,128,256]{3,2,1,0:T(8,128)(2,1)S(1)} all-to-all(bf16[8,2,128,256]{3,2,1,0:T(8,128)(2,1)S(1)} %broadcast_in_dim.112), channel_id=1, replica_groups=mesh['img'=64,'blk'=8] {'blk'}, dimensions={0} | all-to-all | bytes 2097152 | tf_op jit(solution)/shard_map/all_to_all | solution.py:14
  108.1 1.9 collective-permute-start.3
  110.0 3.9 %collective-permute-start.2 = (bf16[16,128,256]{2,1,0:T(8,128)(2,1)S(1)}, bf16[16,128,256]{2,1,0:T(8,128)(2,1)}, u32[]{:S(2)}, u32[]{:S(2)}) collective-permute-start(bf16[16,128,256]{2,1,0:T(8,128)(2,1)S(1)} %bitcast.160), channel_id=1, source_target_pairs={{0,8},{8,16},{16,24},{24,32},{32,40},{40,48},{48,56},{56,64},{64,7... | collective-permute-start | bytes 3145736 | tf_op jit(solution)/shard_map/ppermute | solution.py:33
  115.4 19.2 %collective-permute-done.3 = bf16[16,128,256]{2,1,0:T(8,128)(2,1)S(1)} collective-permute-done((bf16[16,128,256]{2,1,0:T(8,128)(2,1)S(1)}, bf16[16,128,256]{2,1,0:T(8,128)(2,1)S(1)}, u32[]{:S(2)}, u32[]{:S(2)}) %collective-permute-start.3) | collective-permute-done | bytes 1048608 | tf_op jit(solution)/shard_map/ppermute | solution.py:36
  134.5 4.1 %collective-permute-done.2 = bf16[16,128,256]{2,1,0:T(8,128)(2,1)} collective-permute-done((bf16[16,128,256]{2,1,0:T(8,128)(2,1)S(1)}, bf16[16,128,256]{2,1,0:T(8,128)(2,1)}, u32[]{:S(2)}, u32[]{:S(2)}) %collective-permute-start.2) | collective-permute-done | bytes 1048608 | tf_op jit(solution)/shard_map/ppermute | solution.py:33
  138.7 2.9 %pad_maximum_fusion.1 = bf16[48,128,256]{2,1,0:T(8,128)(2,1)} fusion(bf16[16,128,256]{2,1,0:T(8,128)(2,1)S(1)} %collective-permute-done.3, bf16[16,128,256]{2,1,0:T(8,128)(2,1)S(1)} %bitcast.161, bf16[16,128,256]{2,1,0:T(8,128)(2,1)} %collective-permute-done.2), kind=kLoop, calls=%fused_computation.9 | loop fusion | flops 3145728 | bytes 6291456 | tf_op jit(solution)/shard_map/concatenate | solution.py:37
  141.5 2.5 gather_fusion.2
  146.7 7.8 %all_to_all.41 = f32[8,3,1,2,128]{4,3,1,2,0:T(2,128)S(1)} all-to-all(f32[8,3,1,2,128]{4,3,1,2,0:T(2,128)S(1)} %copy.37), channel_id=1, replica_groups=mesh['img'=64,'blk'=8] {'blk'}, dimensions={0} | all-to-all | bytes 49152 | tf_op jit(solution)/shard_map/all_to_all | solution.py:49
  154.5 1.9 collective-permute-start.4
  156.4 3.9 %collective-permute-start.5 = (f32[2,128]{1,0:T(2,128)S(1)}, f32[2,128]{1,0:T(2,128)S(1)}, u32[]{:S(2)}, u32[]{:S(2)}) collective-permute-start(f32[2,128]{1,0:T(2,128)S(1)} %get-tuple-element.28), channel_id=1, source_target_pairs={{0,8},{8,16},{16,24},{24,32},{32,40},{40,48},{48,56},{56,64},{64,7... | collective-permute-start | bytes 3080 | tf_op jit(solution)/shard_map/ppermute | solution.py:56
  160.4 3.6 %collective-permute-done.5 = f32[2,128]{1,0:T(2,128)S(1)} collective-permute-done((f32[2,128]{1,0:T(2,128)S(1)}, f32[2,128]{1,0:T(2,128)S(1)}, u32[]{:S(2)}, u32[]{:S(2)}) %collective-permute-start.5) | collective-permute-done | bytes 1056 | tf_op jit(solution)/shard_map/ppermute | solution.py:56
  164.0 7.7 %all_to_all.42 = f32[8,2,128]{2,1,0:T(2,128)S(1)} all-to-all(f32[8,2,128]{2,1,0:T(2,128)S(1)} %broadcast_in_dim.117), channel_id=1, replica_groups=mesh['img'=64,'blk'=8] {'blk'}, dimensions={0} | all-to-all | bytes 16384 | tf_op jit(solution)/shard_map/all_to_all | solution.py:14
  171.7 1.9 collective-permute-start.7
  173.6 3.9 %collective-permute-start.6 = (f32[16,128]{1,0:T(8,128)S(1)}, f32[16,128]{1,0:T(8,128)S(1)}, u32[]{:S(2)}, u32[]{:S(2)}) collective-permute-start(f32[16,128]{1,0:T(8,128)S(1)} %bitcast.176), channel_id=1, source_target_pairs={{0,8},{8,16},{16,24},{24,32},{32,40},{40,48},{48,56},{56,64},{64,7... | collective-permute-start | bytes 24584 | tf_op jit(solution)/shard_map/ppermute | solution.py:33
  177.5 3.7 %collective-permute-done.6 = f32[16,128]{1,0:T(8,128)S(1)} collective-permute-done((f32[16,128]{1,0:T(8,128)S(1)}, f32[16,128]{1,0:T(8,128)S(1)}, u32[]{:S(2)}, u32[]{:S(2)}) %collective-permute-start.6) | collective-permute-done | bytes 8224 | tf_op jit(solution)/shard_map/ppermute | solution.py:33
  184.2 7.8 %all_to_all.43 = f32[8,3,1,2,128]{4,3,1,2,0:T(2,128)S(1)} all-to-all(f32[8,3,1,2,128]{4,3,1,2,0:T(2,128)S(1)} %copy.38), channel_id=1, replica_groups=mesh['img'=64,'blk'=8] {'blk'}, dimensions={0} | all-to-all | bytes 49152 | tf_op jit(solution)/shard_map/all_to_all | solution.py:49
  192.0 1.9 collective-permute-start.8
  193.9 3.9 %collective-permute-start.9 = (f32[2,128]{1,0:T(2,128)S(1)}, f32[2,128]{1,0:T(2,128)S(1)}, u32[]{:S(2)}, u32[]{:S(2)}) collective-permute-start(f32[2,128]{1,0:T(2,128)S(1)} %get-tuple-element.26), channel_id=1, source_target_pairs={{0,8},{8,16},{16,24},{24,32},{32,40},{40,48},{48,56},{56,64},{64,7... | collective-permute-start | bytes 3080 | tf_op jit(solution)/shard_map/ppermute | solution.py:56
  197.8 3.6 %collective-permute-done.9 = f32[2,128]{1,0:T(2,128)S(1)} collective-permute-done((f32[2,128]{1,0:T(2,128)S(1)}, f32[2,128]{1,0:T(2,128)S(1)}, u32[]{:S(2)}, u32[]{:S(2)}) %collective-permute-start.9) | collective-permute-done | bytes 1056 | tf_op jit(solution)/shard_map/ppermute | solution.py:56
  201.5 7.7 %all_to_all.44 = f32[8,2,128]{2,1,0:T(2,128)S(1)} all-to-all(f32[8,2,128]{2,1,0:T(2,128)S(1)} %broadcast_in_dim.118), channel_id=1, replica_groups=mesh['img'=64,'blk'=8] {'blk'}, dimensions={0} | all-to-all | bytes 16384 | tf_op jit(solution)/shard_map/all_to_all | solution.py:14
  209.2 1.9 collective-permute-start.11
  211.1 3.9 %collective-permute-start.10 = (f32[16,128]{1,0:T(8,128)S(1)}, f32[16,128]{1,0:T(8,128)S(1)}, u32[]{:S(2)}, u32[]{:S(2)}) collective-permute-start(f32[16,128]{1,0:T(8,128)S(1)} %bitcast.179), channel_id=1, source_target_pairs={{0,8},{8,16},{16,24},{24,32},{32,40},{40,48},{48,56},{56,64},{64,7... | collective-permute-start | bytes 24584 | tf_op jit(solution)/shard_map/ppermute | solution.py:33
  215.0 3.7 %collective-permute-done.10 = f32[16,128]{1,0:T(8,128)S(1)} collective-permute-done((f32[16,128]{1,0:T(8,128)S(1)}, f32[16,128]{1,0:T(8,128)S(1)}, u32[]{:S(2)}, u32[]{:S(2)}) %collective-permute-start.10) | collective-permute-done | bytes 8224 | tf_op jit(solution)/shard_map/ppermute | solution.py:33
  222.3 7.8 %all_to_all.45 = f32[8,3,1,2,128]{4,3,1,2,0:T(2,128)S(1)} all-to-all(f32[8,3,1,2,128]{4,3,1,2,0:T(2,128)S(1)} %copy.39), channel_id=1, replica_groups=mesh['img'=64,'blk'=8] {'blk'}, dimensions={0} | all-to-all | bytes 49152 | tf_op jit(solution)/shard_map/all_to_all | solution.py:49
  230.1 1.9 collective-permute-start.12
  232.0 3.9 %collective-permute-start.13 = (f32[2,128]{1,0:T(2,128)S(1)}, f32[2,128]{1,0:T(2,128)S(1)}, u32[]{:S(2)}, u32[]{:S(2)}) collective-permute-start(f32[2,128]{1,0:T(2,128)S(1)} %get-tuple-element.24), channel_id=1, source_target_pairs={{0,8},{8,16},{16,24},{24,32},{32,40},{40,48},{48,56},{56,64},{64,7... | collective-permute-start | bytes 3080 | tf_op jit(solution)/shard_map/ppermute | solution.py:56
  235.9 3.6 %collective-permute-done.13 = f32[2,128]{1,0:T(2,128)S(1)} collective-permute-done((f32[2,128]{1,0:T(2,128)S(1)}, f32[2,128]{1,0:T(2,128)S(1)}, u32[]{:S(2)}, u32[]{:S(2)}) %collective-permute-start.13) | collective-permute-done | bytes 1056 | tf_op jit(solution)/shard_map/ppermute | solution.py:56
  240.2 7.7 %all_to_all.46 = f32[8,2,128]{2,1,0:T(2,128)S(1)} all-to-all(f32[8,2,128]{2,1,0:T(2,128)S(1)} %broadcast_in_dim.119), channel_id=1, replica_groups=mesh['img'=64,'blk'=8] {'blk'}, dimensions={0} | all-to-all | bytes 16384 | tf_op jit(solution)/shard_map/all_to_all | solution.py:14
  247.9 1.9 collective-permute-start.15
  249.8 3.9 %collective-permute-start.14 = (f32[16,128]{1,0:T(8,128)S(1)}, f32[16,128]{1,0:T(8,128)S(1)}, u32[]{:S(2)}, u32[]{:S(2)}) collective-permute-start(f32[16,128]{1,0:T(8,128)S(1)} %bitcast.182), channel_id=1, source_target_pairs={{0,8},{8,16},{16,24},{24,32},{32,40},{40,48},{48,56},{56,64},{64,7... | collective-permute-start | bytes 24584 | tf_op jit(solution)/shard_map/ppermute | solution.py:33
  253.7 3.7 %collective-permute-done.14 = f32[16,128]{1,0:T(8,128)S(1)} collective-permute-done((f32[16,128]{1,0:T(8,128)S(1)}, f32[16,128]{1,0:T(8,128)S(1)}, u32[]{:S(2)}, u32[]{:S(2)}) %collective-permute-start.14) | collective-permute-done | bytes 8224 | tf_op jit(solution)/shard_map/ppermute | solution.py:33
  258.7 1.1 copy.40
  (114 shorter events, 16.5 us)
Async XLA Ops:
  0.6 88.4 %copy-start = (bf16[512,512]{1,0:T(8,128)(2,1)S(1)}, bf16[512,512]{1,0:T(8,128)(2,1)}, u32[]{:S(2)}) copy-start(bf16[512,512]{1,0:T(8,128)(2,1)} %param.21) | copy-start | bytes 1572868
  0.6 7.1 %copy-start.1 = (bf16[2,128,256]{2,1,0:T(8,128)(2,1)S(1)}, bf16[2,128,256]{2,1,0:T(8,128)(2,1)}, u32[]{:S(2)}) copy-start(bf16[2,128,256]{2,1,0:T(8,128)(2,1)} %param.14) | copy-start | bytes 393220
  0.7 6.5 %copy-start.10 = (s32[2,6]{1,0:T(2,128)S(1)}, s32[2,6]{1,0:T(2,128)}, u32[]{:S(2)}) copy-start(s32[2,6]{1,0:T(2,128)} %param.15) | copy-start | bytes 148
  0.7 6.6 %copy-start.6 = (s32[1024]{0:T(1024)S(1)}, s32[1024]{0:T(1024)}, u32[]{:S(2)}) copy-start(s32[1024]{0:T(1024)} %param.17) | copy-start | bytes 12292
  0.7 7.0 %copy-start.13 = (s32[2]{0:T(128)S(1)}, s32[2]{0:T(128)}, u32[]{:S(2)}) copy-start(s32[2]{0:T(128)} %param.16) | copy-start | bytes 28
  0.7 7.0 %copy-start.2 = (bf16[256,256]{1,0:T(8,128)(2,1)S(1)}, bf16[256,256]{1,0:T(8,128)(2,1)}, u32[]{:S(2)}) copy-start(bf16[256,256]{1,0:T(8,128)(2,1)} %param.18) | copy-start | bytes 393220
  0.7 62.5 %copy-start.12 = (bf16[256,256]{1,0:T(8,128)(2,1)S(1)}, bf16[256,256]{1,0:T(8,128)(2,1)}, u32[]{:S(2)}) copy-start(bf16[256,256]{1,0:T(8,128)(2,1)} %param.19) | copy-start | bytes 393220
  2.8 20.3 %all-to-all-start = ((bf16[8,2,128,256]{3,2,1,0:T(8,128)(2,1)}), bf16[8,2,128,256]{3,2,1,0:T(8,128)(2,1)S(1)}, u32[]{:S(2)}, u32[]{:S(2)}) async-start(bf16[8,2,128,256]{3,2,1,0:T(8,128)(2,1)} %broadcast_in_dim.109), calls=%async_computation | async-start | bytes 2097152 | tf_op jit(solution)/shard_map/all_to_all | solution.py:14
  7.1 0.6 copy-start.4
  23.1 33.8 %collective-permute-start.1 = (bf16[16,128,256]{2,1,0:T(8,128)(2,1)S(1)}, bf16[16,128,256]{2,1,0:T(8,128)(2,1)S(1)}, u32[]{:S(2)}, u32[]{:S(2)}) collective-permute-start(bf16[16,128,256]{2,1,0:T(8,128)(2,1)S(1)} %bitcast.165), channel_id=1, source_target_pairs={{8,0},{16,8},{24,16},{32,24},{40,32},{48,40},{56,48},{64,56},{72,6... | collective-permute-start | bytes 3145736 | tf_op jit(solution)/shard_map/ppermute | solution.py:36
  34.7 28.5 %collective-permute-start = (bf16[16,128,256]{2,1,0:T(8,128)(2,1)S(1)}, bf16[16,128,256]{2,1,0:T(8,128)(2,1)}, u32[]{:S(2)}, u32[]{:S(2)}) collective-permute-start(bf16[16,128,256]{2,1,0:T(8,128)(2,1)S(1)} %bitcast.166), channel_id=1, source_target_pairs={{0,8},{8,16},{16,24},{24,32},{32,40},{40,48},{48,56},{56,64},{64,7... | collective-permute-start | bytes 3145736 | tf_op jit(solution)/shard_map/ppermute | solution.py:33
  36.7 0.9 copy-start.8
  77.5 5.8 %copy-start.3 = (bf16[2,128,256]{1,2,0:T(8,128)(2,1)S(1)}, bf16[2,128,256]{1,2,0:T(8,128)(2,1)}, u32[]{:S(2)}) copy-start(bf16[2,128,256]{1,2,0:T(8,128)(2,1)} %copy.34) | copy-start | bytes 393220
  77.5 5.8 %copy-start.7 = (pred[2,768]{1,0:T(4,128)(4,1)S(1)}, pred[2,768]{1,0:T(4,128)(4,1)}, u32[]{:S(2)}) copy-start(pred[2,768]{1,0:T(4,128)(4,1)} %bitcast_and_fusion) | copy-start | bytes 4612
  86.1 2.9 %copy-start.11 = (bf16[512,256]{1,0:T(8,128)(2,1)S(1)}, bf16[512,256]{1,0:T(8,128)(2,1)}, u32[]{:S(2)}) copy-start(bf16[512,256]{1,0:T(8,128)(2,1)} %param.22) | copy-start | bytes 786436
  88.8 25.2 %copy-start.5 = (s32[2,6]{1,0:T(2,128)S(1)}, s32[2,6]{1,0:T(2,128)}, u32[]{:S(2)}) copy-start(s32[2,6]{1,0:T(2,128)} %copy-done.4) | copy-start | bytes 148
  108.1 26.4 %collective-permute-start.3 = (bf16[16,128,256]{2,1,0:T(8,128)(2,1)S(1)}, bf16[16,128,256]{2,1,0:T(8,128)(2,1)S(1)}, u32[]{:S(2)}, u32[]{:S(2)}) collective-permute-start(bf16[16,128,256]{2,1,0:T(8,128)(2,1)S(1)} %bitcast.159), channel_id=1, source_target_pairs={{8,0},{16,8},{24,16},{32,24},{40,32},{48,40},{56,48},{64,56},{72,6... | collective-permute-start | bytes 3145736 | tf_op jit(solution)/shard_map/ppermute | solution.py:36
  110.0 28.6 %collective-permute-start.2 = (bf16[16,128,256]{2,1,0:T(8,128)(2,1)S(1)}, bf16[16,128,256]{2,1,0:T(8,128)(2,1)}, u32[]{:S(2)}, u32[]{:S(2)}) collective-permute-start(bf16[16,128,256]{2,1,0:T(8,128)(2,1)S(1)} %bitcast.160), channel_id=1, source_target_pairs={{0,8},{8,16},{16,24},{24,32},{32,40},{40,48},{48,56},{56,64},{64,7... | collective-permute-start | bytes 3145736 | tf_op jit(solution)/shard_map/ppermute | solution.py:33
  145.6 75.0 %copy-start.9 = (s32[2]{0:T(128)S(1)}, s32[2]{0:T(128)}, u32[]{:S(2)}) copy-start(s32[2]{0:T(128)} %copy-done.8) | copy-start | bytes 28
  154.5 5.9 %collective-permute-start.4 = (f32[2,128]{1,0:T(2,128)S(1)}, f32[2,128]{1,0:T(2,128)S(1)}, u32[]{:S(2)}, u32[]{:S(2)}) collective-permute-start(f32[2,128]{1,0:T(2,128)S(1)} %get-tuple-element.27), channel_id=1, source_target_pairs={{8,0},{16,8},{24,16},{32,24},{40,32},{48,40},{56,48},{64,56},{72,6... | collective-permute-start | bytes 3080 | tf_op jit(solution)/shard_map/ppermute | solution.py:56
  156.4 7.6 %collective-permute-start.5 = (f32[2,128]{1,0:T(2,128)S(1)}, f32[2,128]{1,0:T(2,128)S(1)}, u32[]{:S(2)}, u32[]{:S(2)}) collective-permute-start(f32[2,128]{1,0:T(2,128)S(1)} %get-tuple-element.28), channel_id=1, source_target_pairs={{0,8},{8,16},{16,24},{24,32},{32,40},{40,48},{48,56},{56,64},{64,7... | collective-permute-start | bytes 3080 | tf_op jit(solution)/shard_map/ppermute | solution.py:56
  171.7 5.8 %collective-permute-start.7 = (f32[16,128]{1,0:T(8,128)S(1)}, f32[16,128]{1,0:T(8,128)S(1)}, u32[]{:S(2)}, u32[]{:S(2)}) collective-permute-start(f32[16,128]{1,0:T(8,128)S(1)} %bitcast.175), channel_id=1, source_target_pairs={{8,0},{16,8},{24,16},{32,24},{40,32},{48,40},{56,48},{64,56},{72,6... | collective-permute-start | bytes 24584 | tf_op jit(solution)/shard_map/ppermute | solution.py:36
  173.6 7.7 %collective-permute-start.6 = (f32[16,128]{1,0:T(8,128)S(1)}, f32[16,128]{1,0:T(8,128)S(1)}, u32[]{:S(2)}, u32[]{:S(2)}) collective-permute-start(f32[16,128]{1,0:T(8,128)S(1)} %bitcast.176), channel_id=1, source_target_pairs={{0,8},{8,16},{16,24},{24,32},{32,40},{40,48},{48,56},{56,64},{64,7... | collective-permute-start | bytes 24584 | tf_op jit(solution)/shard_map/ppermute | solution.py:33
  192.0 5.9 %collective-permute-start.8 = (f32[2,128]{1,0:T(2,128)S(1)}, f32[2,128]{1,0:T(2,128)S(1)}, u32[]{:S(2)}, u32[]{:S(2)}) collective-permute-start(f32[2,128]{1,0:T(2,128)S(1)} %get-tuple-element.25), channel_id=1, source_target_pairs={{8,0},{16,8},{24,16},{32,24},{40,32},{48,40},{56,48},{64,56},{72,6... | collective-permute-start | bytes 3080 | tf_op jit(solution)/shard_map/ppermute | solution.py:56
  193.9 7.6 %collective-permute-start.9 = (f32[2,128]{1,0:T(2,128)S(1)}, f32[2,128]{1,0:T(2,128)S(1)}, u32[]{:S(2)}, u32[]{:S(2)}) collective-permute-start(f32[2,128]{1,0:T(2,128)S(1)} %get-tuple-element.26), channel_id=1, source_target_pairs={{0,8},{8,16},{16,24},{24,32},{32,40},{40,48},{48,56},{56,64},{64,7... | collective-permute-start | bytes 3080 | tf_op jit(solution)/shard_map/ppermute | solution.py:56
  209.2 5.8 %collective-permute-start.11 = (f32[16,128]{1,0:T(8,128)S(1)}, f32[16,128]{1,0:T(8,128)S(1)}, u32[]{:S(2)}, u32[]{:S(2)}) collective-permute-start(f32[16,128]{1,0:T(8,128)S(1)} %bitcast.178), channel_id=1, source_target_pairs={{8,0},{16,8},{24,16},{32,24},{40,32},{48,40},{56,48},{64,56},{72,6... | collective-permute-start | bytes 24584 | tf_op jit(solution)/shard_map/ppermute | solution.py:36
  211.1 7.7 %collective-permute-start.10 = (f32[16,128]{1,0:T(8,128)S(1)}, f32[16,128]{1,0:T(8,128)S(1)}, u32[]{:S(2)}, u32[]{:S(2)}) collective-permute-start(f32[16,128]{1,0:T(8,128)S(1)} %bitcast.179), channel_id=1, source_target_pairs={{0,8},{8,16},{16,24},{24,32},{32,40},{40,48},{48,56},{56,64},{64,7... | collective-permute-start | bytes 24584 | tf_op jit(solution)/shard_map/ppermute | solution.py:33
  230.1 5.9 %collective-permute-start.12 = (f32[2,128]{1,0:T(2,128)S(1)}, f32[2,128]{1,0:T(2,128)S(1)}, u32[]{:S(2)}, u32[]{:S(2)}) collective-permute-start(f32[2,128]{1,0:T(2,128)S(1)} %get-tuple-element.23), channel_id=1, source_target_pairs={{8,0},{16,8},{24,16},{32,24},{40,32},{48,40},{56,48},{64,56},{72,6... | collective-permute-start | bytes 3080 | tf_op jit(solution)/shard_map/ppermute | solution.py:56
  232.0 7.6 %collective-permute-start.13 = (f32[2,128]{1,0:T(2,128)S(1)}, f32[2,128]{1,0:T(2,128)S(1)}, u32[]{:S(2)}, u32[]{:S(2)}) collective-permute-start(f32[2,128]{1,0:T(2,128)S(1)} %get-tuple-element.24), channel_id=1, source_target_pairs={{0,8},{8,16},{16,24},{24,32},{32,40},{40,48},{48,56},{56,64},{64,7... | collective-permute-start | bytes 3080 | tf_op jit(solution)/shard_map/ppermute | solution.py:56
  247.9 5.8 %collective-permute-start.15 = (f32[16,128]{1,0:T(8,128)S(1)}, f32[16,128]{1,0:T(8,128)S(1)}, u32[]{:S(2)}, u32[]{:S(2)}) collective-permute-start(f32[16,128]{1,0:T(8,128)S(1)} %bitcast.181), channel_id=1, source_target_pairs={{8,0},{16,8},{24,16},{32,24},{40,32},{48,40},{56,48},{64,56},{72,6... | collective-permute-start | bytes 24584 | tf_op jit(solution)/shard_map/ppermute | solution.py:36
  249.8 7.7 %collective-permute-start.14 = (f32[16,128]{1,0:T(8,128)S(1)}, f32[16,128]{1,0:T(8,128)S(1)}, u32[]{:S(2)}, u32[]{:S(2)}) collective-permute-start(f32[16,128]{1,0:T(8,128)S(1)} %bitcast.182), channel_id=1, source_target_pairs={{0,8},{8,16},{16,24},{24,32},{32,40},{40,48},{48,56},{56,64},{64,7... | collective-permute-start | bytes 24584 | tf_op jit(solution)/shard_map/ppermute | solution.py:33
where the time goes:
time: 261 us; the launch traced here: 260 us
  waiting for transfers between devices  85.2 us (33%)
  blocking collectives  64.8 us (25%)
  starting transfers between devices  58.6 us (22%)
  local copies, waits for them, and re-layouts  20.3 us (8%)
  matrix products  15.5 us (6%)
  other arithmetic  13.3 us (5%)
    all_to_all x4, blocking collectives, copy_for_each(): return lax.all_to_all(copies, axis, split_axis=0, concat_axis=0, tiled=True)  41.5 us
    ppermute x5, waiting for transfers between devices, with_halo(): lax.ppermute(lax.slice_in_dim(block, 0, width, axis=dim), axis, backward)  37.6 us
    all_to_all x3, blocking collectives, summed_on_arrival(): lax.all_to_all(blocks, axis, split_axis=0, concat_axis=0, tiled=True)  23.3 us
    ppermute x5, waiting for transfers between devices, with_halo(): lax.ppermute(lax.slice_in_dim(block, block.shape[dim] - width, None, axis...  21.6 us
    ppermute x5, starting transfers between devices, with_halo(): lax.ppermute(lax.slice_in_dim(block, 0, width, axis=dim), axis, backward)  19.2 us
    ppermute x5, starting transfers between devices, with_halo(): lax.ppermute(lax.slice_in_dim(block, block.shape[dim] - width, None, axis...  17.6 us
    ppermute x6, starting transfers between devices, shifted_2(): return lax.ppermute(block, axis, route)  17.5 us
    all_to_all x1, waiting for transfers between devices, copy_for_each(): return lax.all_to_all(copies, axis, split_axis=0, concat_axis=0, tiled=True)  15.1 us
  transfers between devices with their start and end apart: 17, of which 11 were waited for; matrix products, arithmetic and copies ran while one was open for 1% of the time, Pallas kernels for 0%

commit v1 on v0

v1 whole, which is shorter than its diff:
```python
import functools

import jax
import jax.numpy as jnp
from jax import lax
from jax.experimental import pallas as pl
from jax.experimental.pallas import tpu as pltpu
from jax.sharding import PartitionSpec as P

HEADS = 4
ITERS = 3
BLOCK = 128
D = 256
TILES = 6
GROUP = 16
NEAR = 3 * GROUP
CHUNK = 2 * BLOCK + 16
VMEM = pltpu.VMEM
SMEM = pltpu.SMEM
BF = jnp.bfloat16
F32 = jnp.float32
NT = (((1,), (1,)), ((), ()))


def dot(a, b, dims=(((1,), (0,)), ((), ()))):
    return lax.dot_general(a, b, dims, preferred_element_type=F32)


def lanes(shape):
    return lax.broadcasted_iota(jnp.int32, shape, len(shape) - 1)


def place_of(n, img):
    group = n // GROUP
    j = n % GROUP
    parity = (img + group + 1) % 2
    in_pair = jnp.logical_or(group == 1, group == 2 - 2 * (img % 2))
    chunk = j // 4 + jnp.where(in_pair, 4 * parity, 0)
    return in_pair, (j // 2) % 2, chunk, (j % 2) * BLOCK


def attend_kernel(
    cov_ref, count_ref, kpt_ref, desc_ref, ra, rao, rb, rbo,
    wq_ref, wk_ref, wv_ref, wm_ref, wo_ref, out_ref, tiles, logits, probs,
):
    img = lax.axis_index("img")
    core = lax.axis_index("blk") % 2
    first = (img - 1) * GROUP
    for r in range(2):
        for t in range(TILES):
            n = cov_ref[r, t] - first
            in_pair, its_core, chunk, row = place_of(n, img)
            same = its_core == core
            dst = pl.ds((r * TILES + t) * BLOCK, BLOCK)
            for src, hit in (
                (ra, in_pair & same),
                (rao, in_pair & ~same),
                (rb, ~in_pair & same),
                (rbo, ~in_pair & ~same),
            ):
                @pl.when(hit)
                def _(src=src):
                    tiles[dst, :] = src[chunk, pl.ds(pl.multiple_of(row, BLOCK), BLOCK), :]

    desc = desc_ref[...]
    query = dot(desc, wq_ref[...]).astype(BF) * jnp.asarray(0.125, BF)
    messages = []
    head_of = lanes((BLOCK, D)) // (D // HEADS)
    for r in range(2):
        keys = tiles[pl.ds(r * TILES * BLOCK, TILES * BLOCK), :]
        k = dot(keys, wk_ref[...]).astype(BF)
        v = dot(keys, wv_ref[...]).astype(BF)
        q = query[r * BLOCK : (r + 1) * BLOCK]
        q4 = jnp.concatenate(
            [jnp.where(head_of == h, q, jnp.zeros_like(q)) for h in range(HEADS)], axis=0
        )
        logits[...] = dot(q4, k, NT)
        live = jnp.concatenate(
            [
                lanes((1, BLOCK))
                < jnp.where(t < count_ref[r], kpt_ref[cov_ref[r, t]], 0)
                for t in range(TILES)
            ],
            axis=1,
        )
        for h in range(HEADS):
            rows = pl.ds(h * BLOCK, BLOCK)
            s = jnp.where(live, logits[rows, :], -1e30)
            top = jnp.max(s, axis=1, keepdims=True)
            e = jnp.exp(s - top)
            total = jnp.sum(e, axis=1, keepdims=True)
            probs[rows, :] = (e * (1.0 / total)).astype(BF)
        mixed = dot(probs[...], v)
        message = jnp.zeros((BLOCK, D), F32)
        for h in range(HEADS):
            message = jnp.where(head_of == h, mixed[h * BLOCK : (h + 1) * BLOCK], message)
        messages.append(message.astype(BF))
    message = jnp.concatenate(messages, axis=0)
    hidden = dot(desc, wm_ref[:D, :]) + dot(message, wm_ref[D:, :])
    hidden = jnp.maximum(hidden, 0.0).astype(BF)
    refined = (desc.astype(F32) + dot(hidden, wo_ref[...])).astype(BF)
    for c in range(8):
        out_ref[c] = refined


def row_block(x, k, cov_ref, kpt_ref, blk):
    chip = x // 2
    other = x % 2
    its_core = (blk + other) % 2
    return chip * 4 + its_core * 2 + k


def table(cov_ref, j, t):
    return cov_ref[j * 8 + t]


def column_pass(keep, sums, cov_ref, j, w):
    for t in range(TILES):
        n = table(cov_ref, j, t)
        part = (keep[j * TILES + t] * w).reshape(BLOCK // 8, 8, BLOCK)
        sums[n] += jnp.sum(part, axis=0)


def send_out(sums, core, s_ref, m_ref, f_ref):
    s_ref[...] = jnp.sum(sums[...], axis=1)
    m_ref[...] = s_ref[pl.ds(pl.multiple_of(GROUP * (1 - core), GROUP), 2 * GROUP), :]
    f_ref[...] = s_ref[pl.ds(pl.multiple_of(2 * GROUP * (1 - core), GROUP), GROUP), :]


def build_kernel(
    cov_ref, kpt_ref, dust_ref, ra, rao, rb, rbo,
    keep, top_ref, own_ref, s_ref, m_ref, f_ref, near, sums, raw,
):
    img = lax.axis_index("img")
    blk = lax.axis_index("blk")
    core = blk % 2
    first = (img - 1) * GROUP
    dust = dust_ref[0]
    e = img % 2
    for src, other in ((ra, 0), (rao, 1)):
        for chunk in range(8):
            group = jnp.where(e == 0, 1 + chunk // 4, chunk // 4)
            for k in range(2):
                n = group * GROUP + (chunk % 4) * 4 + ((core + other) % 2) * 2 + k
                near[n] = src[chunk, k * BLOCK : (k + 1) * BLOCK, :]
    for src, other in ((rb, 0), (rbo, 1)):
        for chunk in range(4):
            group = jnp.where(e == 0, 0, 2)
            for k in range(2):
                n = group * GROUP + chunk * 4 + ((core + other) % 2) * 2 + k
                near[n] = src[chunk, k * BLOCK : (k + 1) * BLOCK, :]
    sums[...] = jnp.zeros_like(sums)

    def limit(j, t):
        n = table(cov_ref, j, t)
        return jnp.where(t < table(cov_ref, j, TILES), kpt_ref[first + n], 0)

    def body(j, _):
        mine = near[GROUP + j]
        top = jnp.full((BLOCK, BLOCK), dust, F32)
        for t in range(TILES):
            s = dot(mine, near[table(cov_ref, j, t)], NT) * 0.0625
            s = jnp.where(lanes((BLOCK, BLOCK)) < limit(j, t), s, -1e30)
            raw[t] = s
            top = jnp.maximum(top, s)
        top = jnp.max(top, axis=1, keepdims=True)
        top_ref[j] = jnp.broadcast_to(top, (BLOCK, BLOCK))
        total = jnp.zeros((BLOCK, BLOCK), F32)
        for t in range(TILES):
            k = jnp.exp(raw[t] - top)
            keep[j * TILES + t] = k
            total = total + k
        total = jnp.sum(total, axis=1, keepdims=True) + jnp.exp(dust - top)
        live = lax.broadcasted_iota(jnp.int32, (BLOCK, 1), 0) < kpt_ref[first + GROUP + j]
        w = jnp.broadcast_to(jnp.where(live, 1.0 / total, 0.0), (BLOCK, BLOCK))
        column_pass(keep, sums, cov_ref, j, w)
        return _

    lax.fori_loop(0, GROUP, body, 0)
    for r in range(2):
        j = 2 * blk + r
        for t in range(TILES):
            own_ref[r * TILES + t] = (
                dot(near[GROUP + j], near[table(cov_ref, j, t)], NT) * 0.0625
            )
    send_out(sums, core, s_ref, m_ref, f_ref)


def column_total(core, s_ref, x_ref, y_ref, total):
    total[...] = s_ref[...]
    for ref, c in ((x_ref, core), (y_ref, 1 - core)):
        at = pl.multiple_of(GROUP * c, GROUP)
        total[pl.ds(at, 2 * GROUP), :] += ref[: 2 * GROUP, :]
        at = pl.multiple_of(2 * GROUP * c, GROUP)
        total[pl.ds(at, GROUP), :] += ref[2 * GROUP :, :]


def sweep_kernel(
    last, cov_ref, kpt_ref, dust_ref, keep, top_ref, own_ref, s_in, x_ref, y_ref, *refs
):
    if last:
        s_ref, m_ref, f_ref, base_ref, bin_ref, total, scale, sums = refs
    else:
        s_ref, m_ref, f_ref, total, scale, sums = refs
    img = lax.axis_index("img")
    blk = lax.axis_index("blk")
    core = blk % 2
    first = (img - 1) * GROUP
    dust = dust_ref[0]
    column_total(core, s_in, x_ref, y_ref, total)
    v = 1.0 / (total[...] + jnp.exp(jnp.full((NEAR, BLOCK), dust, F32)))
    scale[...] = jnp.broadcast_to(v[:, None, :], (NEAR, 8, BLOCK))
    sums[...] = jnp.zeros_like(sums)

    def row_total(j):
        part = jnp.zeros((BLOCK // 8, 8, BLOCK), F32)
        for t in range(TILES):
            k = keep[j * TILES + t].reshape(BLOCK // 8, 8, BLOCK)
            part = part + k * scale[table(cov_ref, j, t)][None]
        part = jnp.sum(part.reshape(BLOCK, BLOCK), axis=1, keepdims=True)
        return part + jnp.exp(dust - top_ref[j])

    def body(j, _):
        live = lax.broadcasted_iota(jnp.int32, (BLOCK, BLOCK), 0) < kpt_ref[first + GROUP + j]
        w = jnp.where(live, 1.0 / row_total(j), 0.0)
        column_pass(keep, sums, cov_ref, j, w)
        return _

    lax.fori_loop(0, GROUP, body, 0)
    send_out(sums, core, s_ref, m_ref, f_ref)
    if last:
        eye = lax.broadcasted_iota(jnp.int32, (BLOCK, BLOCK), 0) == lanes((BLOCK, BLOCK))
        for r in range(2):
            j = 2 * blk + r
            row_pot = -(top_ref[j] + jnp.log(row_total(j)))
            for t in range(TILES):
                base_ref[r * TILES + t] = own_ref[r * TILES + t] + row_pot
            flat = jnp.sum(jnp.where(eye, row_pot, 0.0), axis=0, keepdims=True)
            bin_ref[r : r + 1, :] = jnp.where(
                lanes((1, BLOCK)) < kpt_ref[first + GROUP + j], dust + flat, 0.0
            )


def plan_kernel(
    cov_ref, kpt_ref, dust_ref, base_ref, s_in, x_ref, y_ref, plan_hbm, bin_ref, total, pots, plan, sems
):
    img = lax.axis_index("img")
    blk = lax.axis_index("blk")
    first = (img - 1) * GROUP
    dust = dust_ref[0]
    column_total(blk % 2, s_in, x_ref, y_ref, total)
    pot = -jnp.log(total[...] + jnp.exp(jnp.full((NEAR, BLOCK), dust, F32)))
    total[...] = pot
    pots[...] = jnp.broadcast_to(pot[:, None, :], (NEAR, 8, BLOCK))
    copies = []
    for r in range(2):
        j = 2 * blk + r
        rows = lax.broadcasted_iota(jnp.int32, (BLOCK, BLOCK), 0) < kpt_ref[first + GROUP + j]
        for t in range(TILES):
            n = table(cov_ref, j, t)
            limit = jnp.where(t < table(cov_ref, j, TILES), kpt_ref[first + n], 0)
            full = base_ref[r * TILES + t].reshape(BLOCK // 8, 8, BLOCK) + pots[n][None]
            plan[r, t] = jnp.where(
                rows & (lanes((BLOCK, BLOCK)) < limit), full.reshape(BLOCK, BLOCK), 0.0
            )
            copy = pltpu.make_async_copy(
                plan.at[r, t], plan_hbm.at[r, t], sems.at[r * TILES + t]
            )
            copy.start()
            copies.append(copy)
        own = total[pl.ds(GROUP + j, 1), :]
        bin_ref[r : r + 1, :] = jnp.where(
            lanes((1, BLOCK)) < kpt_ref[first + GROUP + j], dust + own, 0.0
        )
    for copy in copies:
        copy.wait()


def swap_cores(x):
    count = lax.axis_size("blk")
    return lax.ppermute(x, "blk", [(b, b ^ 1) for b in range(count)])


def outwards(x, distance):
    imgs, blks = lax.axis_size("img"), lax.axis_size("blk")
    route = []
    for i in range(imgs):
        for b in range(blks):
            to = i + distance * (1 - 2 * (b % 2))
            if 0 <= to < imgs:
                route.append((i * blks + b, to * blks + b))
    return lax.ppermute(x, ("img", "blk"), route)


def pairs(offset):
    imgs, blks = lax.axis_size("img"), lax.axis_size("blk")
    groups = []
    for i in range(offset, imgs + offset, 2):
        for c in range(2):
            groups.append([(k % imgs) * blks + b for k in (i, i + 1) for b in range(c, blks, 2)])
    return groups


def gather_near(copies):
    ra = lax.all_to_all(
        copies, ("img", "blk"), 0, 0, tiled=True, axis_index_groups=pairs(0)
    )
    rao = swap_cores(ra)
    rb = lax.all_to_all(
        copies, ("img", "blk"), 0, 0, tiled=True, axis_index_groups=pairs(1)
    )
    e = lax.axis_index("img") % 2
    rb = lax.dynamic_slice_in_dim(rb, 4 * e, 4, axis=0)
    rbo = swap_cores(rb)
    return ra, rao, rb, rbo


def spread(m, f):
    x = jnp.concatenate([outwards(m, 1), outwards(f, 2)], axis=0)
    return x, swap_cores(x)


def call(kernel, ins, outs, scratch, limit):
    spaces = {"s": SMEM, "v": VMEM, "h": pl.ANY}
    out_specs = [pl.BlockSpec(memory_space=spaces[k]) for k, *_ in outs]
    return pl.pallas_call(
        kernel,
        in_specs=[pl.BlockSpec(memory_space=spaces[k]) for k, _ in ins],
        out_specs=out_specs,
        out_shape=[jax.ShapeDtypeStruct(s, d) for _, s, d in outs],
        scratch_shapes=scratch,
        compiler_params=pltpu.CompilerParams(vmem_limit_bytes=limit << 20),
    )(*[a for _, a in ins])


def on_device(
    descriptors, covisible, tile_counts, keypoints,
    query_weight, key_weight, value_weight, merge_weight, output_weight, dustbin,
):
    img = lax.axis_index("img")
    blk = lax.axis_index("blk")
    flat = descriptors.reshape(2 * BLOCK, D)
    lists = jnp.concatenate([covisible - (img - 1) * GROUP, tile_counts[:, None]], axis=1)
    lists = jnp.pad(lists.astype(BF), ((0, 14), (0, D - TILES - 1)))
    sent = jnp.concatenate([flat, lists], axis=0)
    sent = jnp.broadcast_to(sent[None], (8, CHUNK, D))
    ra, rao, rb, rbo = gather_near(sent)

    (refined,) = call(
        attend_kernel,
        [("s", covisible), ("s", tile_counts), ("s", keypoints), ("v", flat)]
        + [("v", a) for a in (ra, rao, rb, rbo)]
        + [("v", a) for a in (query_weight, key_weight, value_weight, merge_weight, output_weight)],
        [("v", (8, 2 * BLOCK, D), BF)],
        [
            VMEM((2 * TILES * BLOCK, D), BF),
            VMEM((HEADS * BLOCK, TILES * BLOCK), F32),
            VMEM((HEADS * BLOCK, TILES * BLOCK), BF),
        ],
        24,
    )

    e = img % 2
    mine = lax.dynamic_slice(ra, (4 * e, 2 * BLOCK, 0), (4, 2, 8))
    other = lax.dynamic_slice(rao, (4 * e, 2 * BLOCK, 0), (4, 2, 8))
    core = blk % 2
    lists = jnp.where(
        core == 0, jnp.stack([mine, other], axis=1), jnp.stack([other, mine], axis=1)
    )
    lists = lists.astype(F32).astype(jnp.int32).reshape(GROUP * 8)
    smem = [("s", lists), ("s", keypoints), ("s", dustbin)]

    near = gather_near(refined)
    sums = [("v", (NEAR, BLOCK), F32), ("v", (2 * GROUP, BLOCK), F32), ("v", (GROUP, BLOCK), F32)]
    tile = (BLOCK, BLOCK)
    keep, top, own, s, m, f = call(
        build_kernel,
        smem + [("v", a) for a in near],
        [("v", (GROUP * TILES, *tile), F32), ("v", (GROUP, *tile), F32), ("v", (2 * TILES, *tile), F32)]
        + sums,
        [VMEM((NEAR, BLOCK, D), BF), VMEM((NEAR, 8, BLOCK), F32), VMEM((TILES, *tile), F32)],
        24,
    )
    for sweep in range(1, ITERS):
        x, y = spread(m, f)
        last = sweep == ITERS - 1
        more = [("v", (2 * TILES, *tile), F32), ("v", (2, BLOCK), F32)] if last else []
        got = call(
            functools.partial(sweep_kernel, last),
            smem + [("v", a) for a in (keep, top, own, s, x, y)],
            sums + more,
            [VMEM((NEAR, BLOCK), F32), VMEM((NEAR, 8, BLOCK), F32), VMEM((NEAR, 8, BLOCK), F32)],
            16,
        )
        s, m, f = got[:3]
    base, row_bin = got[3:]
    x, y = spread(m, f)
    plan, col_bin = call(
        plan_kernel,
        smem + [("v", a) for a in (base, s, x, y)],
        [("h", (2, TILES, *tile), F32), ("v", (2, BLOCK), F32)],
        [
            VMEM((NEAR, BLOCK), F32),
            VMEM((NEAR, 8, BLOCK), F32),
            VMEM((2, TILES, *tile), F32),
            pltpu.SemaphoreType.DMA((2 * TILES,)),
        ],
        16,
    )
    return plan, row_bin, col_bin


def solution(mesh):
    split = P(("img", "blk"))
    in_specs = (split, split, split, P(), P(), P(), P(), P(), P(), P())
    return jax.shard_map(
        on_device, mesh=mesh, in_specs=in_specs, out_specs=(split, split, split), check_vma=False
    )
```

time: 261 us -> 170 us (0.65)
  waiting for transfers between devices: 85.2 us -> 49 us
  Pallas kernels: 0 us -> 23.5 us
  blocking collectives: 64.8 us -> 41.9 us
  matrix products: 15.5 us -> 0 us
  local copies, waits for them, and re-layouts: 20.3 us -> 5.26 us
  starting transfers between devices: 58.6 us -> 45.2 us
  other arithmetic: 13.3 us -> 2.35 us
    ppermute x16 -> x13, waiting for transfers between devices: 70 us -> 25.5 us  [the longest x6 19.9 us: outwards(): return lax.ppermute(x, ('img', 'blk'), route)]
    ppermute x16 -> x13, starting transfers between devices: 54.3 us -> 25.8 us  [the longest x7 13.7 us: swap_cores(): return lax.ppermute(x, 'blk', [(b, b ^ 1) for b in range(count)])]
    pallas_call x0 -> x5, Pallas kernels: none -> 23.5 us  [call(): pl.pallas_call(kernel, in_specs=[pl.BlockSpec(memory_space=spaces[k]) for...]
    all_to_all x7 -> x2, blocking collectives: 64.8 us -> 41.9 us  [gather_near(): lax.all_to_all(copies, ('img', 'blk'), 0, 0, tiled=True, axis_index_group...]
    all_to_all x1 -> x2, starting transfers between devices: 4.3 us -> 19.4 us  [gather_near(): lax.all_to_all(copies, ('img', 'blk'), 0, 0, tiled=True, axis_index_group...]
    dot_general x9 -> x0, matrix products: 12.7 us -> none  [the longest x3 7.95 us: project_rows(): jnp.dot(values.reshape(-1, values.shape[-1]), weight, preferred_element_t...]
    gather x13 -> x0, local copies, waits for them, and re-layouts: 11.2 us -> none  [the longest x2 3.24 us: on_device(): jnp.take(near_keys, near_ids, axis=0)]
    all_to_all x1 -> x2, waiting for transfers between devices: 15.1 us -> 23.5 us  [gather_near(): lax.all_to_all(copies, ('img', 'blk'), 0, 0, tiled=True, axis_index_group...]
  transfers between devices with their start and end apart: 17 -> 15, of which waited for: 11 -> 13; matrix products, arithmetic and copies ran while one was open for 1% -> 2% of each run, Pallas kernels for 0% -> 0%
where the time goes in v1:
time: 170 us; the launch traced here: 169 us
  waiting for transfers between devices  49 us (29%)
  starting transfers between devices  45.2 us (27%)
  blocking collectives  41.9 us (25%)
  Pallas kernels  23.5 us (14%)
  local copies, waits for them, and re-layouts  5.26 us (3%)
  other arithmetic  2.35 us (1%)
    all_to_all x2, blocking collectives, gather_near(): lax.all_to_all(copies, ('img', 'blk'), 0, 0, tiled=True, axis_index_group...  41.9 us
    all_to_all x2, waiting for transfers between devices, gather_near(): lax.all_to_all(copies, ('img', 'blk'), 0, 0, tiled=True, axis_index_group...  23.5 us
    pallas_call x5, Pallas kernels, call(): pl.pallas_call(kernel, in_specs=[pl.BlockSpec(memory_space=spaces[k]) for...  23.5 us
    ppermute x6, waiting for transfers between devices, outwards(): return lax.ppermute(x, ('img', 'blk'), route)  19.9 us
    all_to_all x2, starting transfers between devices, gather_near(): lax.all_to_all(copies, ('img', 'blk'), 0, 0, tiled=True, axis_index_group...  19.4 us
    ppermute x7, starting transfers between devices, swap_cores(): return lax.ppermute(x, 'blk', [(b, b ^ 1) for b in range(count)])  13.7 us
    ppermute x6, starting transfers between devices, outwards(): return lax.ppermute(x, ('img', 'blk'), route)  12.1 us
    ppermute x7, waiting for transfers between devices, swap_cores(): return lax.ppermute(x, 'blk', [(b, b ^ 1) for b in range(count)])  5.58 us
  transfers between devices with their start and end apart: 15, of which 13 were waited for; matrix products, arithmetic and copies ran while one was open for 2% of the time, Pallas kernels for 0%

profile of v1, /device:TPU:24, one launch (start us, length us, event | category | flops | bytes accessed | tf_op | source)
XLA Modules:
  0.0 168.7 jit_solution(2086146398349442583)
XLA Ops:
  0.6 0.7 convert_bitcast_fusion
  1.3 0.1 copy.15
  1.4 0.7 subtract_convert_fusion
  2.1 0.1 fusion.5
  2.2 0.9 pad_maximum_fusion
  3.1 1.1 broadcast_in_dim.11
  4.2 22.3 %all_to_all.20.ra = bf16[8,272,256]{2,1,0:T(8,128)(2,1)S(1)} all-to-all(bf16[8,272,256]{2,1,0:T(8,128)(2,1)} %broadcast_in_dim.11), channel_id=1, replica_groups={{0,2,4,6,8,10,12,14},{1,3,5,7,9,11,13,15},{16,18,20,22,24,26,28,30},{17..., dimensions={0} | all-to-all | bytes 2228224 | tf_op jit(solution)/shard_map/all_to_all | solution.py:305
  26.5 12.6 %all-to-all-start.1 = ((bf16[8,272,256]{2,1,0:T(8,128)(2,1)}), bf16[8,272,256]{2,1,0:T(8,128)(2,1)}, u32[]{:S(2)}, u32[]{:S(2)}) async-start(bf16[8,272,256]{2,1,0:T(8,128)(2,1)} %broadcast_in_dim.11), calls=%async_computation.1 | async-start | bytes 2228224 | tf_op jit(solution)/shard_map/all_to_all | solution.py:309
  39.1 0.0 copy-start.4
  39.1 0.0 copy-start.7
  39.1 2.1 %collective-permute-start = (bf16[8,272,256]{2,1,0:T(8,128)(2,1)S(1)}, bf16[8,272,256]{2,1,0:T(8,128)(2,1)S(1)}, u32[]{:S(2)}, u32[]{:S(2)}) collective-permute-start(bf16[8,272,256]{2,1,0:T(8,128)(2,1)S(1)} %all_to_all.20.ra), channel_id=1, source_target_pairs={{0,1},{1,0},{2,3},{3,2},{4,5},{5,4},{6,7},{7,6},{8,9},{9,8},{10,11... | collective-permute-start | bytes 3342344 | tf_op jit(solution)/shard_map/ppermute | solution.py:281
  41.2 11.9 %all-to-all-done.1 = bf16[8,272,256]{2,1,0:T(8,128)(2,1)} async-done(((bf16[8,272,256]{2,1,0:T(8,128)(2,1)}), bf16[8,272,256]{2,1,0:T(8,128)(2,1)}, u32[]{:S(2)}, u32[]{:S(2)}) %all-to-all-start.1) | async-done | bytes 1114144 | tf_op jit(solution)/shard_map/all_to_all | solution.py:309
  53.1 1.1 constant_dynamic-slice_fusion.1.rb
  54.2 1.9 %collective-permute-start.1 = (bf16[4,272,256]{2,1,0:T(8,128)(2,1)S(1)}, bf16[4,272,256]{2,1,0:T(8,128)(2,1)S(1)}, u32[]{:S(2)}, u32[]{:S(2)}) collective-permute-start(bf16[4,272,256]{2,1,0:T(8,128)(2,1)S(1)} %constant_dynamic-slice_fusion.1.rb), channel_id=1, source_target_pairs={{0,1},{1,0},{2,3},{3,2},{4,5},{5,4},{6,7},{7,6},{8,9},{9,8},{10,11... | collective-permute-start | bytes 1671176 | tf_op jit(solution)/shard_map/ppermute | solution.py:281
  56.1 1.9 %collective-permute-done.1.rbo = bf16[4,272,256]{2,1,0:T(8,128)(2,1)S(1)} collective-permute-done((bf16[4,272,256]{2,1,0:T(8,128)(2,1)S(1)}, bf16[4,272,256]{2,1,0:T(8,128)(2,1)S(1)}, u32[]{:S(2)}, u32[]{:S(2)}) %collective-permute-start.1) | collective-permute-done | bytes 557088 | tf_op jit(solution)/shard_map/ppermute | solution.py:281
  58.1 5.1 %shard_map.121 = bf16[8,256,256]{2,1,0:T(8,128)(2,1)} custom-call(s32[2,6]{1,0:T(2,128)S(1)} %copy-done.8, s32[2]{0:T(128)S(1)} %copy-done.9, s32[1024]{0:T(1024)S(1)} %copy-done.7, bf16[256,256]{1,0:T(8,128)(2,1)S(1)} %bitcast.8, bf16[8,272,256]{2,1,0:T(8,128)(2,1)S(1)} %all_to_all.20.ra, bf16[8,272,256]{2,1,0:T(8,128)(2,1)S(1)} %collective-permute-done.rao, ...), custom_call_target="tpu_custom_call" | custom-call | tf_op jit(solution)/shard_map/pallas_call | solution.py:326
  63.2 1.0 copy-done
  64.2 19.6 %all_to_all.21.ra = bf16[8,256,256]{2,1,0:T(8,128)(2,1)S(1)} all-to-all(bf16[8,256,256]{2,1,0:T(8,128)(2,1)} %shard_map.121), channel_id=1, replica_groups={{0,2,4,6,8,10,12,14},{1,3,5,7,9,11,13,15},{16,18,20,22,24,26,28,30},{17..., dimensions={0} | all-to-all | bytes 2097152 | tf_op jit(solution)/shard_map/all_to_all | solution.py:305
  83.8 6.8 %all-to-all-start.3 = ((bf16[8,256,256]{2,1,0:T(8,128)(2,1)}), bf16[8,256,256]{2,1,0:T(8,128)(2,1)}, u32[]{:S(2)}, u32[]{:S(2)}) async-start(bf16[8,256,256]{2,1,0:T(8,128)(2,1)} %shard_map.121), calls=%async_computation.3 | async-start | bytes 2097152 | tf_op jit(solution)/shard_map/all_to_all | solution.py:309
  90.6 1.9 %collective-permute-start.2 = (bf16[8,256,256]{2,1,0:T(8,128)(2,1)S(1)}, bf16[8,256,256]{2,1,0:T(8,128)(2,1)}, u32[]{:S(2)}, u32[]{:S(2)}) collective-permute-start(bf16[8,256,256]{2,1,0:T(8,128)(2,1)S(1)} %all_to_all.21.ra), channel_id=1, source_target_pairs={{0,1},{1,0},{2,3},{3,2},{4,5},{5,4},{6,7},{7,6},{8,9},{9,8},{10,11... | collective-permute-start | bytes 3145736 | tf_op jit(solution)/shard_map/ppermute | solution.py:281
  92.5 11.6 %all-to-all-done.3 = bf16[8,256,256]{2,1,0:T(8,128)(2,1)} async-done(((bf16[8,256,256]{2,1,0:T(8,128)(2,1)}), bf16[8,256,256]{2,1,0:T(8,128)(2,1)}, u32[]{:S(2)}, u32[]{:S(2)}) %all-to-all-start.3) | async-done | bytes 1048608 | tf_op jit(solution)/shard_map/all_to_all | solution.py:309
  104.1 1.1 constant_dynamic-slice_fusion.rb
  105.2 1.9 %collective-permute-start.3 = (bf16[4,256,256]{2,1,0:T(8,128)(2,1)S(1)}, bf16[4,256,256]{2,1,0:T(8,128)(2,1)S(1)}, u32[]{:S(2)}, u32[]{:S(2)}) collective-permute-start(bf16[4,256,256]{2,1,0:T(8,128)(2,1)S(1)} %constant_dynamic-slice_fusion.rb), channel_id=1, source_target_pairs={{0,1},{1,0},{2,3},{3,2},{4,5},{5,4},{6,7},{7,6},{8,9},{9,8},{10,11... | collective-permute-start | bytes 1572872 | tf_op jit(solution)/shard_map/ppermute | solution.py:281
  107.8 0.7 dynamic-slice_bitcast_fusion
  108.6 0.1 convert_element_type.17.cov_ref
  108.7 0.3 collective-permute-done.3.rbo
  109.0 9.6 %shard_map.122 = (f32[96,128,128]{2,1,0:T(8,128)S(1)}, f32[16,128,128]{2,1,0:T(8,128)S(1)}, f32[12,128,128]{2,1,0:T(8,128)S(1)}, f32[48,128]{1,0:T(8,128)S(1)}, ...) custom-call(s32[128]{0:T(128)S(1)} %convert_element_type.17.cov_ref, s32[1024]{0:T(1024)S(1)} %copy-done.7, ...), custom_call_target="tpu_custom_call" | custom-call | tf_op jit(solution)/shard_map/pallas_call | solution.py:326
  118.6 1.9 %collective-permute-start.4 = (f32[32,128]{1,0:T(8,128)S(1)}, f32[32,128]{1,0:T(8,128)S(1)}, u32[]{:S(2)}, u32[]{:S(2)}) collective-permute-start(f32[32,128]{1,0:T(8,128)S(1)} %get-tuple-element.23), channel_id=1, source_target_pairs={{0,8},{2,10},{4,12},{6,14},{8,16},{9,1},{10,18},{11,3},{12,20},{13... | collective-permute-start | bytes 49160 | tf_op jit(solution)/shard_map/ppermute | solution.py:292
  120.5 1.9 %collective-permute-start.5 = (f32[16,128]{1,0:T(8,128)S(1)}, f32[16,128]{1,0:T(8,128)S(1)}, u32[]{:S(2)}, u32[]{:S(2)}) collective-permute-start(f32[16,128]{1,0:T(8,128)S(1)} %get-tuple-element.24), channel_id=1, source_target_pairs={{0,16},{2,18},{4,20},{6,22},{8,24},{10,26},{12,28},{14,30},{16,32}... | collective-permute-start | bytes 24584 | tf_op jit(solution)/shard_map/ppermute | solution.py:292
  122.5 3.9 %collective-permute-done.4 = f32[32,128]{1,0:T(8,128)S(1)} collective-permute-done((f32[32,128]{1,0:T(8,128)S(1)}, f32[32,128]{1,0:T(8,128)S(1)}, u32[]{:S(2)}, u32[]{:S(2)}) %collective-permute-start.4) | collective-permute-done | bytes 16416 | tf_op jit(solution)/shard_map/ppermute | solution.py:292
  126.3 2.8 %collective-permute-done.5 = f32[16,128]{1,0:T(8,128)S(1)} collective-permute-done((f32[16,128]{1,0:T(8,128)S(1)}, f32[16,128]{1,0:T(8,128)S(1)}, u32[]{:S(2)}, u32[]{:S(2)}) %collective-permute-start.5) | collective-permute-done | bytes 8224 | tf_op jit(solution)/shard_map/ppermute | solution.py:292
  129.1 2.1 %collective-permute-start.6 = (f32[48,128]{1,0:T(8,128)S(1)}, f32[48,128]{1,0:T(8,128)S(1)}, u32[]{:S(2)}, u32[]{:S(2)}) collective-permute-start(f32[48,128]{1,0:T(8,128)S(1)} %constant_dynamic-update-slice_fusion.x_ref), channel_id=1, source_target_pairs={{0,1},{1,0},{2,3},{3,2},{4,5},{5,4},{6,7},{7,6},{8,9},{9,8},{10,11... | collective-permute-start | bytes 73736 | tf_op jit(solution)/shard_map/ppermute | solution.py:281
  131.2 1.0 collective-permute-done.6.y_ref
  132.2 2.9 %shard_map.123 = (f32[48,128]{1,0:T(8,128)S(1)}, f32[32,128]{1,0:T(8,128)S(1)}, f32[16,128]{1,0:T(8,128)S(1)}) custom-call(s32[128]{0:T(128)S(1)} %convert_element_type.17.cov_ref, s32[1024]{0:T(1024)S(1)} %copy-done.7, f32[1]{0:T(128)S(6)} %copy.24.dust_ref, f32[96,128,128]{2,1,0:T(8,128)S(1)} %get-tuple-element.19.keep, ...), custom_call_target="tpu_custom_call" | custom-call | tf_op jit(solution)/shard_map/pallas_call | solution.py:326
  135.1 2.5 %collective-permute-start.7 = (f32[32,128]{1,0:T(8,128)S(1)}, f32[32,128]{1,0:T(8,128)S(1)}, u32[]{:S(2)}, u32[]{:S(2)}) collective-permute-start(f32[32,128]{1,0:T(8,128)S(1)} %get-tuple-element.26), channel_id=1, source_target_pairs={{0,8},{2,10},{4,12},{6,14},{8,16},{9,1},{10,18},{11,3},{12,20},{13... | collective-permute-start | bytes 49160 | tf_op jit(solution)/shard_map/ppermute | solution.py:292
  137.6 1.9 %collective-permute-start.8 = (f32[16,128]{1,0:T(8,128)S(1)}, f32[16,128]{1,0:T(8,128)S(1)}, u32[]{:S(2)}, u32[]{:S(2)}) collective-permute-start(f32[16,128]{1,0:T(8,128)S(1)} %get-tuple-element.27), channel_id=1, source_target_pairs={{0,16},{2,18},{4,20},{6,22},{8,24},{10,26},{12,28},{14,30},{16,32}... | collective-permute-start | bytes 24584 | tf_op jit(solution)/shard_map/ppermute | solution.py:292
  139.5 3.4 %collective-permute-done.7 = f32[32,128]{1,0:T(8,128)S(1)} collective-permute-done((f32[32,128]{1,0:T(8,128)S(1)}, f32[32,128]{1,0:T(8,128)S(1)}, u32[]{:S(2)}, u32[]{:S(2)}) %collective-permute-start.7) | collective-permute-done | bytes 16416 | tf_op jit(solution)/shard_map/ppermute | solution.py:292
  142.9 3.3 %collective-permute-done.8 = f32[16,128]{1,0:T(8,128)S(1)} collective-permute-done((f32[16,128]{1,0:T(8,128)S(1)}, f32[16,128]{1,0:T(8,128)S(1)}, u32[]{:S(2)}, u32[]{:S(2)}) %collective-permute-start.8) | collective-permute-done | bytes 8224 | tf_op jit(solution)/shard_map/ppermute | solution.py:292
  146.1 1.9 %collective-permute-start.9 = (f32[48,128]{1,0:T(8,128)S(1)}, f32[48,128]{1,0:T(8,128)S(1)}, u32[]{:S(2)}, u32[]{:S(2)}) collective-permute-start(f32[48,128]{1,0:T(8,128)S(1)} %constant_dynamic-update-slice_fusion.2.x_ref), channel_id=1, source_target_pairs={{0,1},{1,0},{2,3},{3,2},{4,5},{5,4},{6,7},{7,6},{8,9},{9,8},{10,11... | collective-permute-start | bytes 73736 | tf_op jit(solution)/shard_map/ppermute | solution.py:281
  148.1 1.2 collective-permute-done.9.y_ref
  149.2 3.7 %shard_map.124 = (f32[48,128]{1,0:T(8,128)S(1)}, f32[32,128]{1,0:T(8,128)S(1)}, f32[16,128]{1,0:T(8,128)S(1)}, f32[12,128,128]{2,1,0:T(8,128)S(1)}, f32[2,128]{1,0:T(2,128)}) custom-call(s32[128]{0:T(128)S(1)} %convert_element_type.17.cov_ref, s32[1024]{0:T(1024)S(1)} %copy-done.7, f32[1]{0:T(128)S(6)} %copy.24.dust_ref, ...), custom_call_target="tpu_custom_call" | custom-call | tf_op jit(solution)/shard_map/pallas_call | solution.py:326
  152.9 1.9 %collective-permute-start.10 = (f32[32,128]{1,0:T(8,128)S(1)}, f32[32,128]{1,0:T(8,128)S(1)}, u32[]{:S(2)}, u32[]{:S(2)}) collective-permute-start(f32[32,128]{1,0:T(8,128)S(1)} %get-tuple-element.30), channel_id=1, source_target_pairs={{0,8},{2,10},{4,12},{6,14},{8,16},{9,1},{10,18},{11,3},{12,20},{13... | collective-permute-start | bytes 49160 | tf_op jit(solution)/shard_map/ppermute | solution.py:292
  154.9 1.9 %collective-permute-start.11 = (f32[16,128]{1,0:T(8,128)S(1)}, f32[16,128]{1,0:T(8,128)S(1)}, u32[]{:S(2)}, u32[]{:S(2)}) collective-permute-start(f32[16,128]{1,0:T(8,128)S(1)} %get-tuple-element.31), channel_id=1, source_target_pairs={{0,16},{2,18},{4,20},{6,22},{8,24},{10,26},{12,28},{14,30},{16,32}... | collective-permute-start | bytes 24584 | tf_op jit(solution)/shard_map/ppermute | solution.py:292
  156.8 3.9 %collective-permute-done.10 = f32[32,128]{1,0:T(8,128)S(1)} collective-permute-done((f32[32,128]{1,0:T(8,128)S(1)}, f32[32,128]{1,0:T(8,128)S(1)}, u32[]{:S(2)}, u32[]{:S(2)}) %collective-permute-start.10) | collective-permute-done | bytes 16416 | tf_op jit(solution)/shard_map/ppermute | solution.py:292
  160.7 2.8 %collective-permute-done.11 = f32[16,128]{1,0:T(8,128)S(1)} collective-permute-done((f32[16,128]{1,0:T(8,128)S(1)}, f32[16,128]{1,0:T(8,128)S(1)}, u32[]{:S(2)}, u32[]{:S(2)}) %collective-permute-start.11) | collective-permute-done | bytes 8224 | tf_op jit(solution)/shard_map/ppermute | solution.py:292
  163.4 1.9 %collective-permute-start.12 = (f32[48,128]{1,0:T(8,128)S(1)}, f32[48,128]{1,0:T(8,128)S(1)}, u32[]{:S(2)}, u32[]{:S(2)}) collective-permute-start(f32[48,128]{1,0:T(8,128)S(1)} %constant_dynamic-update-slice_fusion.4.x_ref), channel_id=1, source_target_pairs={{0,1},{1,0},{2,3},{3,2},{4,5},{5,4},{6,7},{7,6},{8,9},{9,8},{10,11... | collective-permute-start | bytes 73736 | tf_op jit(solution)/shard_map/ppermute | solution.py:281
  165.3 1.2 collective-permute-done.12.y_ref
  166.5 2.2 %shard_map.125 = (f32[2,6,128,128]{3,2,1,0:T(8,128)}, f32[2,128]{1,0:T(2,128)}) custom-call(s32[128]{0:T(128)S(1)} %convert_element_type.17.cov_ref, s32[1024]{0:T(1024)S(1)} %copy-done.7, f32[1]{0:T(128)S(6)} %copy.24.dust_ref, f32[12,128,128]{2,1,0:T(8,128)S(1)} %get-tuple-element.28.base_ref, f32[48,128]{1,0:T(8,128)S(1)} %get-tuple-element.29.s_in, ...), custom_call_target="tpu_custom_call" | custom-call | tf_op jit(solution)/shard_map/pallas_call | solution.py:326
  (30 shorter events, 0.1 us)
Async XLA Ops:
  26.5 31.6 %copy-start.5 = (bf16[256,256]{1,0:T(8,128)(2,1)S(1)}, bf16[256,256]{1,0:T(8,128)(2,1)}, u32[]{:S(2)}) copy-start(bf16[256,256]{1,0:T(8,128)(2,1)} %wk_ref.1) | copy-start | bytes 393220
  26.5 31.6 %copy-start.6 = (bf16[256,256]{1,0:T(8,128)(2,1)S(1)}, bf16[256,256]{1,0:T(8,128)(2,1)}, u32[]{:S(2)}) copy-start(bf16[256,256]{1,0:T(8,128)(2,1)} %wv_ref.1) | copy-start | bytes 393220
  26.5 26.6 %all-to-all-start.1 = ((bf16[8,272,256]{2,1,0:T(8,128)(2,1)}), bf16[8,272,256]{2,1,0:T(8,128)(2,1)}, u32[]{:S(2)}, u32[]{:S(2)}) async-start(bf16[8,272,256]{2,1,0:T(8,128)(2,1)} %broadcast_in_dim.11), calls=%async_computation.1 | async-start | bytes 2228224 | tf_op jit(solution)/shard_map/all_to_all | solution.py:309
  39.1 19.0 %copy-start.1 = (bf16[2,128,256]{2,1,0:T(8,128)(2,1)S(1)}, bf16[2,128,256]{2,1,0:T(8,128)(2,1)}, u32[]{:S(2)}) copy-start(bf16[2,128,256]{2,1,0:T(8,128)(2,1)} %param.10) | copy-start | bytes 393220
  39.1 19.0 %copy-start.2 = (bf16[512,512]{1,0:T(8,128)(2,1)S(1)}, bf16[512,512]{1,0:T(8,128)(2,1)}, u32[]{:S(2)}) copy-start(bf16[512,512]{1,0:T(8,128)(2,1)} %wm_ref.1) | copy-start | bytes 1572868
  39.1 19.0 %copy-start.3 = (bf16[512,256]{1,0:T(8,128)(2,1)S(1)}, bf16[512,256]{1,0:T(8,128)(2,1)}, u32[]{:S(2)}) copy-start(bf16[512,256]{1,0:T(8,128)(2,1)} %wo_ref.1) | copy-start | bytes 786436
  39.1 19.0 %copy-start.4 = (bf16[256,256]{1,0:T(8,128)(2,1)S(1)}, bf16[256,256]{1,0:T(8,128)(2,1)}, u32[]{:S(2)}) copy-start(bf16[256,256]{1,0:T(8,128)(2,1)} %wq_ref.1) | copy-start | bytes 393220
  39.1 19.0 %copy-start.7 = (s32[1024]{0:T(1024)S(1)}, s32[1024]{0:T(1024)}, u32[]{:S(2)}) copy-start(s32[1024]{0:T(1024)} %kpt_ref.9) | copy-start | bytes 12292
  39.1 19.0 %copy-start.8 = (s32[2,6]{1,0:T(2,128)S(1)}, s32[2,6]{1,0:T(2,128)}, u32[]{:S(2)}) copy-start(s32[2,6]{1,0:T(2,128)} %cov_ref.1) | copy-start | bytes 148
  39.1 19.0 %copy-start.9 = (s32[2]{0:T(128)S(1)}, s32[2]{0:T(128)}, u32[]{:S(2)}) copy-start(s32[2]{0:T(128)} %count_ref.1) | copy-start | bytes 28
  39.1 18.9 %collective-permute-start = (bf16[8,272,256]{2,1,0:T(8,128)(2,1)S(1)}, bf16[8,272,256]{2,1,0:T(8,128)(2,1)S(1)}, u32[]{:S(2)}, u32[]{:S(2)}) collective-permute-start(bf16[8,272,256]{2,1,0:T(8,128)(2,1)S(1)} %all_to_all.20.ra), channel_id=1, source_target_pairs={{0,1},{1,0},{2,3},{3,2},{4,5},{5,4},{6,7},{7,6},{8,9},{9,8},{10,11... | collective-permute-start | bytes 3342344 | tf_op jit(solution)/shard_map/ppermute | solution.py:281
  54.2 3.9 %collective-permute-start.1 = (bf16[4,272,256]{2,1,0:T(8,128)(2,1)S(1)}, bf16[4,272,256]{2,1,0:T(8,128)(2,1)S(1)}, u32[]{:S(2)}, u32[]{:S(2)}) collective-permute-start(bf16[4,272,256]{2,1,0:T(8,128)(2,1)S(1)} %constant_dynamic-slice_fusion.1.rb), channel_id=1, source_target_pairs={{0,1},{1,0},{2,3},{3,2},{4,5},{5,4},{6,7},{7,6},{8,9},{9,8},{10,11... | collective-permute-start | bytes 1671176 | tf_op jit(solution)/shard_map/ppermute | solution.py:281
  63.2 1.0 copy-start
  83.8 20.3 %all-to-all-start.3 = ((bf16[8,256,256]{2,1,0:T(8,128)(2,1)}), bf16[8,256,256]{2,1,0:T(8,128)(2,1)}, u32[]{:S(2)}, u32[]{:S(2)}) async-start(bf16[8,256,256]{2,1,0:T(8,128)(2,1)} %shard_map.121), calls=%async_computation.3 | async-start | bytes 2097152 | tf_op jit(solution)/shard_map/all_to_all | solution.py:309
  90.6 18.4 %collective-permute-start.2 = (bf16[8,256,256]{2,1,0:T(8,128)(2,1)S(1)}, bf16[8,256,256]{2,1,0:T(8,128)(2,1)}, u32[]{:S(2)}, u32[]{:S(2)}) collective-permute-start(bf16[8,256,256]{2,1,0:T(8,128)(2,1)S(1)} %all_to_all.21.ra), channel_id=1, source_target_pairs={{0,1},{1,0},{2,3},{3,2},{4,5},{5,4},{6,7},{7,6},{8,9},{9,8},{10,11... | collective-permute-start | bytes 3145736 | tf_op jit(solution)/shard_map/ppermute | solution.py:281
  105.2 3.8 %collective-permute-start.3 = (bf16[4,256,256]{2,1,0:T(8,128)(2,1)S(1)}, bf16[4,256,256]{2,1,0:T(8,128)(2,1)S(1)}, u32[]{:S(2)}, u32[]{:S(2)}) collective-permute-start(bf16[4,256,256]{2,1,0:T(8,128)(2,1)S(1)} %constant_dynamic-slice_fusion.rb), channel_id=1, source_target_pairs={{0,1},{1,0},{2,3},{3,2},{4,5},{5,4},{6,7},{7,6},{8,9},{9,8},{10,11... | collective-permute-start | bytes 1572872 | tf_op jit(solution)/shard_map/ppermute | solution.py:281
  118.6 7.7 %collective-permute-start.4 = (f32[32,128]{1,0:T(8,128)S(1)}, f32[32,128]{1,0:T(8,128)S(1)}, u32[]{:S(2)}, u32[]{:S(2)}) collective-permute-start(f32[32,128]{1,0:T(8,128)S(1)} %get-tuple-element.23), channel_id=1, source_target_pairs={{0,8},{2,10},{4,12},{6,14},{8,16},{9,1},{10,18},{11,3},{12,20},{13... | collective-permute-start | bytes 49160 | tf_op jit(solution)/shard_map/ppermute | solution.py:292
  120.5 8.6 %collective-permute-start.5 = (f32[16,128]{1,0:T(8,128)S(1)}, f32[16,128]{1,0:T(8,128)S(1)}, u32[]{:S(2)}, u32[]{:S(2)}) collective-permute-start(f32[16,128]{1,0:T(8,128)S(1)} %get-tuple-element.24), channel_id=1, source_target_pairs={{0,16},{2,18},{4,20},{6,22},{8,24},{10,26},{12,28},{14,30},{16,32}... | collective-permute-start | bytes 24584 | tf_op jit(solution)/shard_map/ppermute | solution.py:292
  129.1 3.1 %collective-permute-start.6 = (f32[48,128]{1,0:T(8,128)S(1)}, f32[48,128]{1,0:T(8,128)S(1)}, u32[]{:S(2)}, u32[]{:S(2)}) collective-permute-start(f32[48,128]{1,0:T(8,128)S(1)} %constant_dynamic-update-slice_fusion.x_ref), channel_id=1, source_target_pairs={{0,1},{1,0},{2,3},{3,2},{4,5},{5,4},{6,7},{7,6},{8,9},{9,8},{10,11... | collective-permute-start | bytes 73736 | tf_op jit(solution)/shard_map/ppermute | solution.py:281
  135.1 7.7 %collective-permute-start.7 = (f32[32,128]{1,0:T(8,128)S(1)}, f32[32,128]{1,0:T(8,128)S(1)}, u32[]{:S(2)}, u32[]{:S(2)}) collective-permute-start(f32[32,128]{1,0:T(8,128)S(1)} %get-tuple-element.26), channel_id=1, source_target_pairs={{0,8},{2,10},{4,12},{6,14},{8,16},{9,1},{10,18},{11,3},{12,20},{13... | collective-permute-start | bytes 49160 | tf_op jit(solution)/shard_map/ppermute | solution.py:292
  137.6 8.6 %collective-permute-start.8 = (f32[16,128]{1,0:T(8,128)S(1)}, f32[16,128]{1,0:T(8,128)S(1)}, u32[]{:S(2)}, u32[]{:S(2)}) collective-permute-start(f32[16,128]{1,0:T(8,128)S(1)} %get-tuple-element.27), channel_id=1, source_target_pairs={{0,16},{2,18},{4,20},{6,22},{8,24},{10,26},{12,28},{14,30},{16,32}... | collective-permute-start | bytes 24584 | tf_op jit(solution)/shard_map/ppermute | solution.py:292
  146.1 3.1 %collective-permute-start.9 = (f32[48,128]{1,0:T(8,128)S(1)}, f32[48,128]{1,0:T(8,128)S(1)}, u32[]{:S(2)}, u32[]{:S(2)}) collective-permute-start(f32[48,128]{1,0:T(8,128)S(1)} %constant_dynamic-update-slice_fusion.2.x_ref), channel_id=1, source_target_pairs={{0,1},{1,0},{2,3},{3,2},{4,5},{5,4},{6,7},{7,6},{8,9},{9,8},{10,11... | collective-permute-start | bytes 73736 | tf_op jit(solution)/shard_map/ppermute | solution.py:281
  152.9 7.7 %collective-permute-start.10 = (f32[32,128]{1,0:T(8,128)S(1)}, f32[32,128]{1,0:T(8,128)S(1)}, u32[]{:S(2)}, u32[]{:S(2)}) collective-permute-start(f32[32,128]{1,0:T(8,128)S(1)} %get-tuple-element.30), channel_id=1, source_target_pairs={{0,8},{2,10},{4,12},{6,14},{8,16},{9,1},{10,18},{11,3},{12,20},{13... | collective-permute-start | bytes 49160 | tf_op jit(solution)/shard_map/ppermute | solution.py:292
  154.9 8.6 %collective-permute-start.11 = (f32[16,128]{1,0:T(8,128)S(1)}, f32[16,128]{1,0:T(8,128)S(1)}, u32[]{:S(2)}, u32[]{:S(2)}) collective-permute-start(f32[16,128]{1,0:T(8,128)S(1)} %get-tuple-element.31), channel_id=1, source_target_pairs={{0,16},{2,18},{4,20},{6,22},{8,24},{10,26},{12,28},{14,30},{16,32}... | collective-permute-start | bytes 24584 | tf_op jit(solution)/shard_map/ppermute | solution.py:292
  163.4 3.1 %collective-permute-start.12 = (f32[48,128]{1,0:T(8,128)S(1)}, f32[48,128]{1,0:T(8,128)S(1)}, u32[]{:S(2)}, u32[]{:S(2)}) collective-permute-start(f32[48,128]{1,0:T(8,128)S(1)} %constant_dynamic-update-slice_fusion.4.x_ref), channel_id=1, source_target_pairs={{0,1},{1,0},{2,3},{3,2},{4,5},{5,4},{6,7},{7,6},{8,9},{9,8},{10,11... | collective-permute-start | bytes 73736 | tf_op jit(solution)/shard_map/ppermute | solution.py:281

commit v2 on v1

--- a/solution.py
+++ b/solution.py
@@ -30,37 +30,42 @@
     return lax.broadcasted_iota(jnp.int32, shape, len(shape) - 1)
 
 
-def place_of(n, img):
-    group = n // GROUP
-    j = n % GROUP
-    parity = (img + group + 1) % 2
-    in_pair = jnp.logical_or(group == 1, group == 2 - 2 * (img % 2))
-    chunk = j // 4 + jnp.where(in_pair, 4 * parity, 0)
-    return in_pair, (j // 2) % 2, chunk, (j % 2) * BLOCK
+def pack_kernel(cov_ref, count_ref, desc_ref, out_ref):
+    first = (lax.axis_index("img") - 1) * GROUP
+    rows = lax.broadcasted_iota(jnp.int32, (16, D), 0)
+    at = lanes((16, D))
+    lists = jnp.zeros((16, D), F32)
+    for r in range(2):
+        for t in range(TILES + 1):
+            value = count_ref[r] if t == TILES else cov_ref[r, t] - first
+            lists = jnp.where((rows == r) & (at == t), value.astype(F32), lists)
+    for c in range(4):
+        out_ref[c, : 2 * BLOCK, :] = desc_ref[...]
+        out_ref[c, 2 * BLOCK :, :] = lists.astype(BF)
 
 
 def attend_kernel(
-    cov_ref, count_ref, kpt_ref, desc_ref, ra, rao, rb, rbo,
-    wq_ref, wk_ref, wv_ref, wm_ref, wo_ref, out_ref, tiles, logits, probs,
+    cov_ref, count_ref, kpt_ref, desc_ref, own, own_o, low, low_o, high, high_o,
+    wq_ref, wk_ref, wv_ref, wm_ref, wo_ref, out_ref, lists_ref, tiles, logits, probs,
 ):
     img = lax.axis_index("img")
     core = lax.axis_index("blk") % 2
     first = (img - 1) * GROUP
+    for src, its_core in ((own, core), (own_o, 1 - core)):
+        for x in range(4):
+            lists = src[x, 2 * BLOCK :, :BLOCK].astype(F32).astype(jnp.int32)
+            lists_ref[pl.ds(4 * x + 2 * its_core, 2), :] = lists[:2]
     for r in range(2):
         for t in range(TILES):
             n = cov_ref[r, t] - first
-            in_pair, its_core, chunk, row = place_of(n, img)
-            same = its_core == core
+            group, chip, row = n // GROUP, n % GROUP // 4, n % 2 * BLOCK
+            same = n // 2 % 2 == core
             dst = pl.ds((r * TILES + t) * BLOCK, BLOCK)
-            for src, hit in (
-                (ra, in_pair & same),
-                (rao, in_pair & ~same),
-                (rb, ~in_pair & same),
-                (rbo, ~in_pair & ~same),
-            ):
-                @pl.when(hit)
-                def _(src=src):
-                    tiles[dst, :] = src[chunk, pl.ds(pl.multiple_of(row, BLOCK), BLOCK), :]
+            for g, pair in enumerate(((low, low_o), (own, own_o), (high, high_o))):
+                for src, hit in zip(pair, (same, ~same)):
+                    @pl.when((group == g) & hit)
+                    def _(src=src):
+                        tiles[dst, :] = src[chip, pl.ds(pl.multiple_of(row, BLOCK), BLOCK), :]
 
     desc = desc_ref[...]
     query = dot(desc, wq_ref[...]).astype(BF) * jnp.asarray(0.125, BF)
@@ -99,19 +104,12 @@
     hidden = dot(desc, wm_ref[:D, :]) + dot(message, wm_ref[D:, :])
     hidden = jnp.maximum(hidden, 0.0).astype(BF)
     refined = (desc.astype(F32) + dot(hidden, wo_ref[...])).astype(BF)
-    for c in range(8):
+    for c in range(4):
         out_ref[c] = refined
 
 
-def row_block(x, k, cov_ref, kpt_ref, blk):
-    chip = x // 2
-    other = x % 2
-    its_core = (blk + other) % 2
-    return chip * 4 + its_core * 2 + k
-
-
-def table(cov_ref, j, t):
-    return cov_ref[j * 8 + t]
+def table(lists_ref, j, t):
+    return lists_ref[j, t]
 
 
 def column_pass(keep, sums, cov_ref, j, w):
@@ -121,34 +119,51 @@
         sums[n] += jnp.sum(part, axis=0)
 
 
-def send_out(sums, core, s_ref, m_ref, f_ref):
-    s_ref[...] = jnp.sum(sums[...], axis=1)
-    m_ref[...] = s_ref[pl.ds(pl.multiple_of(GROUP * (1 - core), GROUP), 2 * GROUP), :]
-    f_ref[...] = s_ref[pl.ds(pl.multiple_of(2 * GROUP * (1 - core), GROUP), GROUP), :]
+def rank(img, core):
+    return (img + 2 * core) % 4
+
+
+def send_out(sums, flat, s_ref, m_ref):
+    s = jnp.sum(sums[...], axis=1)
+    s_ref[...] = s
+    flat[:NEAR, :] = s
+    me = rank(lax.axis_index("img"), lax.axis_index("blk") % 2)
+    for k in range(4):
+        ahead = jnp.clip(k - me, 0, 2)
+        m_ref[k] = flat[pl.ds(pl.multiple_of(GROUP * ahead, GROUP), 2 * GROUP), :]
+
+
+def column_total(s_ref, x_ref, y_ref, total):
+    img = lax.axis_index("img")
+    total[...] = s_ref[...]
+    for ref, core in ((x_ref, lax.axis_index("blk") % 2), (y_ref, 1 - lax.axis_index("blk") % 2)):
+        me = rank(img, core)
+        for side, there in ((1, me < 2), (-1, me >= 2)):
+            near_at, far_at = (GROUP, 2 * GROUP) if side > 0 else (0, 0)
+
+            @pl.when(there & (img + side >= 0) & (img + side < lax.axis_size("img")))
+            def _():
+                total[near_at : near_at + 2 * GROUP, :] += ref[me + side]
+
+            @pl.when(there & (img + 2 * side >= 0) & (img + 2 * side < lax.axis_size("img")))
+            def _():
+                total[far_at : far_at + GROUP, :] += ref[me + 2 * side, :GROUP, :]
 
 
 def build_kernel(
-    cov_ref, kpt_ref, dust_ref, ra, rao, rb, rbo,
-    keep, top_ref, own_ref, s_ref, m_ref, f_ref, near, sums, raw,
+    cov_ref, kpt_ref, dust_ref, own, own_o, low, low_o, high, high_o,
+    keep, top_ref, own_ref, s_ref, m_ref, near, sums, flat, raw,
 ):
     img = lax.axis_index("img")
     blk = lax.axis_index("blk")
     core = blk % 2
     first = (img - 1) * GROUP
     dust = dust_ref[0]
-    e = img % 2
-    for src, other in ((ra, 0), (rao, 1)):
-        for chunk in range(8):
-            group = jnp.where(e == 0, 1 + chunk // 4, chunk // 4)
-            for k in range(2):
-                n = group * GROUP + (chunk % 4) * 4 + ((core + other) % 2) * 2 + k
-                near[n] = src[chunk, k * BLOCK : (k + 1) * BLOCK, :]
-    for src, other in ((rb, 0), (rbo, 1)):
-        for chunk in range(4):
-            group = jnp.where(e == 0, 0, 2)
-            for k in range(2):
-                n = group * GROUP + chunk * 4 + ((core + other) % 2) * 2 + k
-                near[n] = src[chunk, k * BLOCK : (k + 1) * BLOCK, :]
+    for g, pair in enumerate(((low, low_o), (own, own_o), (high, high_o))):
+        for src, its_core in zip(pair, (core, 1 - core)):
+            for x in range(4):
+                for k in range(2):
+                    near[GROUP * g + 4 * x + 2 * its_core + k] = src[x, k * BLOCK : (k + 1) * BLOCK, :]
     sums[...] = jnp.zeros_like(sums)
 
     def limit(j, t):
@@ -183,31 +198,21 @@
             own_ref[r * TILES + t] = (
                 dot(near[GROUP + j], near[table(cov_ref, j, t)], NT) * 0.0625
             )
-    send_out(sums, core, s_ref, m_ref, f_ref)
-
-
-def column_total(core, s_ref, x_ref, y_ref, total):
-    total[...] = s_ref[...]
-    for ref, c in ((x_ref, core), (y_ref, 1 - core)):
-        at = pl.multiple_of(GROUP * c, GROUP)
-        total[pl.ds(at, 2 * GROUP), :] += ref[: 2 * GROUP, :]
-        at = pl.multiple_of(2 * GROUP * c, GROUP)
-        total[pl.ds(at, GROUP), :] += ref[2 * GROUP :, :]
+    send_out(sums, flat, s_ref, m_ref)
 
 
 def sweep_kernel(
     last, cov_ref, kpt_ref, dust_ref, keep, top_ref, own_ref, s_in, x_ref, y_ref, *refs
 ):
     if last:
-        s_ref, m_ref, f_ref, base_ref, bin_ref, total, scale, sums = refs
+        s_ref, m_ref, base_ref, bin_ref, total, scale, sums, flat = refs
     else:
-        s_ref, m_ref, f_ref, total, scale, sums = refs
+        s_ref, m_ref, total, scale, sums, flat = refs
     img = lax.axis_index("img")
     blk = lax.axis_index("blk")
-    core = blk % 2
     first = (img - 1) * GROUP
     dust = dust_ref[0]
-    column_total(core, s_in, x_ref, y_ref, total)
+    column_total(s_in, x_ref, y_ref, total)
     v = 1.0 / (total[...] + jnp.exp(jnp.full((NEAR, BLOCK), dust, F32)))
     scale[...] = jnp.broadcast_to(v[:, None, :], (NEAR, 8, BLOCK))
     sums[...] = jnp.zeros_like(sums)
@@ -227,7 +232,7 @@
         return _
 
     lax.fori_loop(0, GROUP, body, 0)
-    send_out(sums, core, s_ref, m_ref, f_ref)
+    send_out(sums, flat, s_ref, m_ref)
     if last:
         eye = lax.broadcasted_iota(jnp.int32, (BLOCK, BLOCK), 0) == lanes((BLOCK, BLOCK))
         for r in range(2):
@@ -248,7 +253,7 @@
     blk = lax.axis_index("blk")
     first = (img - 1) * GROUP
     dust = dust_ref[0]
-    column_total(blk % 2, s_in, x_ref, y_ref, total)
+    column_total(s_in, x_ref, y_ref, total)
     pot = -jnp.log(total[...] + jnp.exp(jnp.full((NEAR, BLOCK), dust, F32)))
     total[...] = pot
     pots[...] = jnp.broadcast_to(pot[:, None, :], (NEAR, 8, BLOCK))
@@ -281,42 +286,28 @@
     return lax.ppermute(x, "blk", [(b, b ^ 1) for b in range(count)])
 
 
-def outwards(x, distance):
+def shifted(x, distance):
+    count = lax.axis_size("img")
+    route = [(i, i + distance) for i in range(count) if 0 <= i + distance < count]
+    return lax.ppermute(x, "img", route)
+
+
+def gather_near(copies):
+    blks = lax.axis_size("blk")
+    groups = [list(range(c, blks, 2)) for c in range(2)]
+    own = lax.all_to_all(copies, "blk", 0, 0, tiled=True, axis_index_groups=groups)
+    low = shifted(own, 1)
+    high = shifted(own, -1)
+    return own, swap_cores(own), low, swap_cores(low), high, swap_cores(high)
+
+
+def exchange(m):
     imgs, blks = lax.axis_size("img"), lax.axis_size("blk")
-    route = []
-    for i in range(imgs):
-        for b in range(blks):
-            to = i + distance * (1 - 2 * (b % 2))
-            if 0 <= to < imgs:
-                route.append((i * blks + b, to * blks + b))
-    return lax.ppermute(x, ("img", "blk"), route)
-
-
-def pairs(offset):
-    imgs, blks = lax.axis_size("img"), lax.axis_size("blk")
-    groups = []
-    for i in range(offset, imgs + offset, 2):
-        for c in range(2):
-            groups.append([(k % imgs) * blks + b for k in (i, i + 1) for b in range(c, blks, 2)])
-    return groups
-
-
-def gather_near(copies):
-    ra = lax.all_to_all(
-        copies, ("img", "blk"), 0, 0, tiled=True, axis_index_groups=pairs(0)
-    )
-    rao = swap_cores(ra)
-    rb = lax.all_to_all(
-        copies, ("img", "blk"), 0, 0, tiled=True, axis_index_groups=pairs(1)
-    )
-    e = lax.axis_index("img") % 2
-    rb = lax.dynamic_slice_in_dim(rb, 4 * e, 4, axis=0)
-    rbo = swap_cores(rb)
-    return ra, rao, rb, rbo
-
-
-def spread(m, f):
-    x = jnp.concatenate([outwards(m, 1), outwards(f, 2)], axis=0)
+    windows = []
+    for b in range(blks):
+        for i in range(2 * (b % 2), imgs + 2 * (b % 2), 4):
+            windows.append([k % imgs * blks + b for k in range(i, i + 4)])
+    x = lax.all_to_all(m, ("img", "blk"), 0, 0, tiled=True, axis_index_groups=windows)
     return x, swap_cores(x)
 
 
@@ -337,21 +328,20 @@
     descriptors, covisible, tile_counts, keypoints,
     query_weight, key_weight, value_weight, merge_weight, output_weight, dustbin,
 ):
-    img = lax.axis_index("img")
-    blk = lax.axis_index("blk")
     flat = descriptors.reshape(2 * BLOCK, D)
-    lists = jnp.concatenate([covisible - (img - 1) * GROUP, tile_counts[:, None]], axis=1)
-    lists = jnp.pad(lists.astype(BF), ((0, 14), (0, D - TILES - 1)))
-    sent = jnp.concatenate([flat, lists], axis=0)
-    sent = jnp.broadcast_to(sent[None], (8, CHUNK, D))
-    ra, rao, rb, rbo = gather_near(sent)
-
-    (refined,) = call(
+    (sent,) = call(
+        pack_kernel,
+        [("s", covisible), ("s", tile_counts), ("v", flat)],
+        [("v", (4, CHUNK, D), BF)],
+        [],
+        4,
+    )
+    refined, lists = call(
         attend_kernel,
         [("s", covisible), ("s", tile_counts), ("s", keypoints), ("v", flat)]
-        + [("v", a) for a in (ra, rao, rb, rbo)]
+        + [("v", a) for a in gather_near(sent)]
         + [("v", a) for a in (query_weight, key_weight, value_weight, merge_weight, output_weight)],
-        [("v", (8, 2 * BLOCK, D), BF)],
+        [("v", (4, 2 * BLOCK, D), BF), ("v", (GROUP, BLOCK), jnp.int32)],
         [
             VMEM((2 * TILES * BLOCK, D), BF),
             VMEM((HEADS * BLOCK, TILES * BLOCK), F32),
@@ -359,42 +349,32 @@
         ],
         24,
     )
-
-    e = img % 2
-    mine = lax.dynamic_slice(ra, (4 * e, 2 * BLOCK, 0), (4, 2, 8))
-    other = lax.dynamic_slice(rao, (4 * e, 2 * BLOCK, 0), (4, 2, 8))
-    core = blk % 2
-    lists = jnp.where(
-        core == 0, jnp.stack([mine, other], axis=1), jnp.stack([other, mine], axis=1)
-    )
-    lists = lists.astype(F32).astype(jnp.int32).reshape(GROUP * 8)
     smem = [("s", lists), ("s", keypoints), ("s", dustbin)]
-
-    near = gather_near(refined)
-    sums = [("v", (NEAR, BLOCK), F32), ("v", (2 * GROUP, BLOCK), F32), ("v", (GROUP, BLOCK), F32)]
+    sums = [("v", (NEAR, BLOCK), F32), ("v", (4, 2 * GROUP, BLOCK), F32)]
     tile = (BLOCK, BLOCK)
-    keep, top, own, s, m, f = call(
+    summing = [VMEM((NEAR, 8, BLOCK), F32), VMEM((NEAR + GROUP, BLOCK), F32)]
+    keep, top, own, s, m = call(
         build_kernel,
-        smem + [("v", a) for a in near],
+        smem + [("v", a) for a in gather_near(refined)],
         [("v", (GROUP * TILES, *tile), F32), ("v", (GROUP, *tile), F32), ("v", (2 * TILES, *tile), F32)]
         + sums,
-        [VMEM((NEAR, BLOCK, D), BF), VMEM((NEAR, 8, BLOCK), F32), VMEM((TILES, *tile), F32)],
+        [VMEM((NEAR, BLOCK, D), BF), *summing, VMEM((TILES, *tile), F32)],
         24,
     )
     for sweep in range(1, ITERS):
-        x, y = spread(m, f)
+        x, y = exchange(m)
         last = sweep == ITERS - 1
         more = [("v", (2 * TILES, *tile), F32), ("v", (2, BLOCK), F32)] if last else []
         got = call(
             functools.partial(sweep_kernel, last),
             smem + [("v", a) for a in (keep, top, own, s, x, y)],
             sums + more,
-            [VMEM((NEAR, BLOCK), F32), VMEM((NEAR, 8, BLOCK), F32), VMEM((NEAR, 8, BLOCK), F32)],
+            [VMEM((NEAR, BLOCK), F32), VMEM((NEAR, 8, BLOCK), F32), *summing],
             16,
         )
-        s, m, f = got[:3]
-    base, row_bin = got[3:]
-    x, y = spread(m, f)
+        s, m = got[:2]
+    base, row_bin = got[2:]
+    x, y = exchange(m)
     plan, col_bin = call(
         plan_kernel,
         smem + [("v", a) for a in (base, s, x, y)],

time: 170 us -> 154 us (0.906); the launches traced: 169 us -> 151 us
  waiting for transfers between devices: 49 us -> 26.4 us
  blocking collectives: 41.9 us -> 50.8 us
  starting transfers between devices: 45.2 us -> 39.2 us
  local copies, waits for them, and re-layouts: 5.26 us -> 9.86 us
  other arithmetic: 2.35 us -> 0 us
    all_to_all x2 -> x0, waiting for transfers between devices: 23.5 us -> none  [gather_near(): lax.all_to_all(copies, ('img', 'blk'), 0, 0, tiled=True, axis_index_group...]
    all_to_all x2 -> x0, starting transfers between devices: 19.4 us -> none  [gather_near(): lax.all_to_all(copies, ('img', 'blk'), 0, 0, tiled=True, axis_index_group...]
    all_to_all x2 -> x5, blocking collectives: 41.9 us -> 50.8 us  [the longest x2 26.4 us: gather_near(): lax.all_to_all(copies, 'blk', 0, 0, tiled=True, axis_index_groups=groups)]
    unnamed x23 -> x26, local copies, waits for them, and re-layouts: 1.07 us -> 9.86 us
    ppermute x6 -> x4, starting transfers between devices: 12.1 us -> 19.3 us  [shifted(): return lax.ppermute(x, 'img', route)]
    ppermute x7 -> x9, starting transfers between devices: 13.7 us -> 19.9 us  [swap_cores(): return lax.ppermute(x, 'blk', [(b, b ^ 1) for b in range(count)])]
    dynamic_slice x2 -> x0, local copies, waits for them, and re-layouts: 2.17 us -> none  [gather_near(): rb = lax.dynamic_slice_in_dim(rb, 4 * e, 4, axis=0)]
    ppermute x6 -> x4, waiting for transfers between devices: 19.9 us -> 20.6 us  [shifted(): return lax.ppermute(x, 'img', route)]
  transfers between devices with their start and end apart: 15 -> 13, of which waited for: 13 -> 9; matrix products, arithmetic and copies ran while one was open for 2% -> 0% of each run, Pallas kernels for 0% -> 0%
where the time goes in v2:
time: 154 us; the launch traced here: 151 us
  blocking collectives  50.8 us (33%)
  starting transfers between devices  39.2 us (25%)
  waiting for transfers between devices  26.4 us (17%)
  Pallas kernels  23.2 us (15%)
  local copies, waits for them, and re-layouts  9.86 us (6%)
    all_to_all x2, blocking collectives, gather_near(): lax.all_to_all(copies, 'blk', 0, 0, tiled=True, axis_index_groups=groups)  26.4 us
    all_to_all x3, blocking collectives, exchange(): lax.all_to_all(m, ('img', 'blk'), 0, 0, tiled=True, axis_index_groups=win...  24.4 us
    pallas_call x6, Pallas kernels, call(): pl.pallas_call(kernel, in_specs=[pl.BlockSpec(memory_space=spaces[k]) for...  23.2 us
    ppermute x4, waiting for transfers between devices, shifted(): return lax.ppermute(x, 'img', route)  20.6 us
    ppermute x9, starting transfers between devices, swap_cores(): return lax.ppermute(x, 'blk', [(b, b ^ 1) for b in range(count)])  19.9 us
    ppermute x4, starting transfers between devices, shifted(): return lax.ppermute(x, 'img', route)  19.3 us
    unnamed x26, local copies, waits for them, and re-layouts  9.86 us
    ppermute x9, waiting for transfers between devices, swap_cores(): return lax.ppermute(x, 'blk', [(b, b ^ 1) for b in range(count)])  5.85 us
  transfers between devices with their start and end apart: 13, of which 9 were waited for; matrix products, arithmetic and copies ran while one was open for 0% of the time, Pallas kernels for 0%

profile of v2, /device:TPU:24, one launch (start us, length us, event | category | flops | bytes accessed | tf_op | source)
XLA Modules:
  0.0 151.0 jit_solution(18232966020128168624)
XLA Ops:
  0.6 0.0 copy-start.1
  0.6 0.9 copy-done.1
  1.5 0.7 copy-done.9
  2.2 0.7 copy-done.11
  2.9 0.6 shard_map.121
  3.5 13.9 %all_to_all.25.own = bf16[4,272,256]{2,1,0:T(8,128)(2,1)S(1)} all-to-all(bf16[4,272,256]{2,1,0:T(8,128)(2,1)S(1)} %shard_map.121), channel_id=1, replica_groups={{0,2,4,6},{1,3,5,7},{8,10,12,14},{9,11,13,15},{16,18,20,22},{17,19,21,2..., dimensions={0} | all-to-all | bytes 1114112 | tf_op jit(solution)/shard_map/all_to_all | solution.py:298
  17.4 11.6 %collective-permute-start.3 = (bf16[4,272,256]{2,1,0:T(8,128)(2,1)S(1)}, bf16[4,272,256]{2,1,0:T(8,128)(2,1)S(1)}, u32[]{:S(2)}, u32[]{:S(2)}) collective-permute-start(bf16[4,272,256]{2,1,0:T(8,128)(2,1)S(1)} %all_to_all.25.own), channel_id=1, source_target_pairs={{8,0},{16,8},{24,16},{32,24},{40,32},{48,40},{56,48},{64,56},{72,6... | collective-permute-start | bytes 1671176 | tf_op jit(solution)/shard_map/ppermute | solution.py:292
  29.0 1.9 %collective-permute-start.1 = (bf16[4,272,256]{2,1,0:T(8,128)(2,1)S(1)}, bf16[4,272,256]{2,1,0:T(8,128)(2,1)S(1)}, u32[]{:S(2)}, u32[]{:S(2)}) collective-permute-start(bf16[4,272,256]{2,1,0:T(8,128)(2,1)S(1)} %all_to_all.25.own), channel_id=1, source_target_pairs={{0,8},{8,16},{16,24},{24,32},{32,40},{40,48},{48,56},{56,64},{64,7... | collective-permute-start | bytes 1671176 | tf_op jit(solution)/shard_map/ppermute | solution.py:292
  30.9 1.9 %collective-permute-start = (bf16[4,272,256]{2,1,0:T(8,128)(2,1)S(1)}, bf16[4,272,256]{2,1,0:T(8,128)(2,1)S(1)}, u32[]{:S(2)}, u32[]{:S(2)}) collective-permute-start(bf16[4,272,256]{2,1,0:T(8,128)(2,1)S(1)} %all_to_all.25.own), channel_id=1, source_target_pairs={{0,1},{1,0},{2,3},{3,2},{4,5},{5,4},{6,7},{7,6},{8,9},{9,8},{10,11... | collective-permute-start | bytes 1671176 | tf_op jit(solution)/shard_map/ppermute | solution.py:286
  32.8 6.6 %collective-permute-done.3.high = bf16[4,272,256]{2,1,0:T(8,128)(2,1)S(1)} collective-permute-done((bf16[4,272,256]{2,1,0:T(8,128)(2,1)S(1)}, bf16[4,272,256]{2,1,0:T(8,128)(2,1)S(1)}, u32[]{:S(2)}, u32[]{:S(2)}) %collective-permute-start.3) | collective-permute-done | bytes 557088 | tf_op jit(solution)/shard_map/ppermute | solution.py:292
  39.4 1.9 %collective-permute-start.4 = (bf16[4,272,256]{2,1,0:T(8,128)(2,1)S(1)}, bf16[4,272,256]{2,1,0:T(8,128)(2,1)S(1)}, u32[]{:S(2)}, u32[]{:S(2)}) collective-permute-start(bf16[4,272,256]{2,1,0:T(8,128)(2,1)S(1)} %collective-permute-done.3.high), channel_id=1, source_target_pairs={{0,1},{1,0},{2,3},{3,2},{4,5},{5,4},{6,7},{7,6},{8,9},{9,8},{10,11... | collective-permute-start | bytes 1671176 | tf_op jit(solution)/shard_map/ppermute | solution.py:286
  41.3 4.3 %collective-permute-done.1.low = bf16[4,272,256]{2,1,0:T(8,128)(2,1)S(1)} collective-permute-done((bf16[4,272,256]{2,1,0:T(8,128)(2,1)S(1)}, bf16[4,272,256]{2,1,0:T(8,128)(2,1)S(1)}, u32[]{:S(2)}, u32[]{:S(2)}) %collective-permute-start.1) | collective-permute-done | bytes 557088 | tf_op jit(solution)/shard_map/ppermute | solution.py:292
  45.6 1.9 %collective-permute-start.2 = (bf16[4,272,256]{2,1,0:T(8,128)(2,1)S(1)}, bf16[4,272,256]{2,1,0:T(8,128)(2,1)S(1)}, u32[]{:S(2)}, u32[]{:S(2)}) collective-permute-start(bf16[4,272,256]{2,1,0:T(8,128)(2,1)S(1)} %collective-permute-done.1.low), channel_id=1, source_target_pairs={{0,1},{1,0},{2,3},{3,2},{4,5},{5,4},{6,7},{7,6},{8,9},{9,8},{10,11... | collective-permute-start | bytes 1671176 | tf_op jit(solution)/shard_map/ppermute | solution.py:286
  47.6 0.0 collective-permute-done.own_o
  47.6 0.0 collective-permute-done.4.high_o
  47.6 1.9 %collective-permute-done.2.low_o = bf16[4,272,256]{2,1,0:T(8,128)(2,1)S(1)} collective-permute-done((bf16[4,272,256]{2,1,0:T(8,128)(2,1)S(1)}, bf16[4,272,256]{2,1,0:T(8,128)(2,1)S(1)}, u32[]{:S(2)}, u32[]{:S(2)}) %collective-permute-start.2) | collective-permute-done | bytes 557088 | tf_op jit(solution)/shard_map/ppermute | solution.py:286
  49.5 1.0 copy-done
  50.5 0.9 copy-done.2
  51.4 0.9 copy-done.3
  52.4 0.9 copy-done.4
  53.3 0.9 copy-done.5
  54.2 0.9 copy-done.6
  55.1 0.7 copy-done.7
  55.8 0.7 copy-done.10
  56.5 0.7 copy-done.12
  57.1 4.2 %shard_map.122 = (bf16[4,256,256]{2,1,0:T(8,128)(2,1)S(1)}, s32[16,128]{1,0:T(8,128)S(1)}) custom-call(s32[2,6]{1,0:T(2,128)S(1)} %copy-done.10, s32[2]{0:T(128)S(1)} %copy-done.12, s32[1024]{0:T(1024)S(1)} %copy-done.7, bf16[256,256]{1,0:T(8,128)(2,1)S(1)} %bitcast.2, bf16[4,272,256]{2,1,0:T(8,128)(2,1)S(1)} %all_to_all.25.own, ...), custom_call_target="tpu_custom_call" | custom-call | tf_op jit(solution)/shard_map/pallas_call | solution.py:317
  61.4 12.5 %all_to_all.26.own = bf16[4,256,256]{2,1,0:T(8,128)(2,1)S(1)} all-to-all(bf16[4,256,256]{2,1,0:T(8,128)(2,1)S(1)} %get-tuple-element.19), channel_id=1, replica_groups={{0,2,4,6},{1,3,5,7},{8,10,12,14},{9,11,13,15},{16,18,20,22},{17,19,21,2..., dimensions={0} | all-to-all | bytes 1048576 | tf_op jit(solution)/shard_map/all_to_all | solution.py:298
  73.8 2.6 %collective-permute-start.8 = (bf16[4,256,256]{2,1,0:T(8,128)(2,1)S(1)}, bf16[4,256,256]{2,1,0:T(8,128)(2,1)S(1)}, u32[]{:S(2)}, u32[]{:S(2)}) collective-permute-start(bf16[4,256,256]{2,1,0:T(8,128)(2,1)S(1)} %all_to_all.26.own), channel_id=1, source_target_pairs={{8,0},{16,8},{24,16},{32,24},{40,32},{48,40},{56,48},{64,56},{72,6... | collective-permute-start | bytes 1572872 | tf_op jit(solution)/shard_map/ppermute | solution.py:292
  76.4 3.3 %collective-permute-start.6 = (bf16[4,256,256]{2,1,0:T(8,128)(2,1)S(1)}, bf16[4,256,256]{2,1,0:T(8,128)(2,1)S(1)}, u32[]{:S(2)}, u32[]{:S(2)}) collective-permute-start(bf16[4,256,256]{2,1,0:T(8,128)(2,1)S(1)} %all_to_all.26.own), channel_id=1, source_target_pairs={{0,8},{8,16},{16,24},{24,32},{32,40},{40,48},{48,56},{56,64},{64,7... | collective-permute-start | bytes 1572872 | tf_op jit(solution)/shard_map/ppermute | solution.py:292
  79.7 1.9 %collective-permute-start.5 = (bf16[4,256,256]{2,1,0:T(8,128)(2,1)S(1)}, bf16[4,256,256]{2,1,0:T(8,128)(2,1)S(1)}, u32[]{:S(2)}, u32[]{:S(2)}) collective-permute-start(bf16[4,256,256]{2,1,0:T(8,128)(2,1)S(1)} %all_to_all.26.own), channel_id=1, source_target_pairs={{0,1},{1,0},{2,3},{3,2},{4,5},{5,4},{6,7},{7,6},{8,9},{9,8},{10,11... | collective-permute-start | bytes 1572872 | tf_op jit(solution)/shard_map/ppermute | solution.py:286
  81.6 7.2 %collective-permute-done.8.high = bf16[4,256,256]{2,1,0:T(8,128)(2,1)S(1)} collective-permute-done((bf16[4,256,256]{2,1,0:T(8,128)(2,1)S(1)}, bf16[4,256,256]{2,1,0:T(8,128)(2,1)S(1)}, u32[]{:S(2)}, u32[]{:S(2)}) %collective-permute-start.8) | collective-permute-done | bytes 524320 | tf_op jit(solution)/shard_map/ppermute | solution.py:292
  88.8 1.9 %collective-permute-start.9 = (bf16[4,256,256]{2,1,0:T(8,128)(2,1)S(1)}, bf16[4,256,256]{2,1,0:T(8,128)(2,1)S(1)}, u32[]{:S(2)}, u32[]{:S(2)}) collective-permute-start(bf16[4,256,256]{2,1,0:T(8,128)(2,1)S(1)} %collective-permute-done.8.high), channel_id=1, source_target_pairs={{0,1},{1,0},{2,3},{3,2},{4,5},{5,4},{6,7},{7,6},{8,9},{9,8},{10,11... | collective-permute-start | bytes 1572872 | tf_op jit(solution)/shard_map/ppermute | solution.py:286
  90.7 2.5 %collective-permute-done.6.low = bf16[4,256,256]{2,1,0:T(8,128)(2,1)S(1)} collective-permute-done((bf16[4,256,256]{2,1,0:T(8,128)(2,1)S(1)}, bf16[4,256,256]{2,1,0:T(8,128)(2,1)S(1)}, u32[]{:S(2)}, u32[]{:S(2)}) %collective-permute-start.6) | collective-permute-done | bytes 524320 | tf_op jit(solution)/shard_map/ppermute | solution.py:292
  93.2 1.9 %collective-permute-start.7 = (bf16[4,256,256]{2,1,0:T(8,128)(2,1)S(1)}, bf16[4,256,256]{2,1,0:T(8,128)(2,1)S(1)}, u32[]{:S(2)}, u32[]{:S(2)}) collective-permute-start(bf16[4,256,256]{2,1,0:T(8,128)(2,1)S(1)} %collective-permute-done.6.low), channel_id=1, source_target_pairs={{0,1},{1,0},{2,3},{3,2},{4,5},{5,4},{6,7},{7,6},{8,9},{9,8},{10,11... | collective-permute-start | bytes 1572872 | tf_op jit(solution)/shard_map/ppermute | solution.py:286
  95.8 1.2 collective-permute-done.7.low_o
  97.0 9.0 %shard_map.123 = (f32[96,128,128]{2,1,0:T(8,128)S(1)}, f32[16,128,128]{2,1,0:T(8,128)S(1)}, f32[12,128,128]{2,1,0:T(8,128)S(1)}, f32[48,128]{1,0:T(8,128)S(1)}, f32[4,32,128]{2,1,0:T(8,128)S(1)}) custom-call(s32[16,128]{1,0:T(8,128)S(1)} %get-tuple-element.18.cov_ref, s32[1024]{0:T(1024)S(1)} %copy-done.8, f32[1]{0:T(128)S(6)} %copy.13.dust_ref, ...), custom_call_target="tpu_custom_call" | custom-call | tf_op jit(solution)/shard_map/pallas_call | solution.py:317
  106.0 8.1 %all_to_all.27.x_ref = f32[4,32,128]{2,1,0:T(8,128)S(1)} all-to-all(f32[4,32,128]{2,1,0:T(8,128)S(1)} %get-tuple-element.24), channel_id=1, replica_groups={{0,8,16,24},{32,40,48,56},{64,72,80,88},{96,104,112,120},{128,136,144,1..., dimensions={0} | all-to-all | bytes 131072 | tf_op jit(solution)/shard_map/all_to_all | solution.py:310
  114.2 2.2 %collective-permute-start.10 = (f32[4,32,128]{2,1,0:T(8,128)S(1)}, f32[4,32,128]{2,1,0:T(8,128)S(1)}, u32[]{:S(2)}, u32[]{:S(2)}) collective-permute-start(f32[4,32,128]{2,1,0:T(8,128)S(1)} %all_to_all.27.x_ref), channel_id=1, source_target_pairs={{0,1},{1,0},{2,3},{3,2},{4,5},{5,4},{6,7},{7,6},{8,9},{9,8},{10,11... | collective-permute-start | bytes 196616 | tf_op jit(solution)/shard_map/ppermute | solution.py:286
  116.3 1.0 collective-permute-done.10.y_ref
  117.3 3.1 %shard_map.124 = (f32[48,128]{1,0:T(8,128)S(1)}, f32[4,32,128]{2,1,0:T(8,128)S(1)}) custom-call(s32[16,128]{1,0:T(8,128)S(1)} %get-tuple-element.18.cov_ref, s32[1024]{0:T(1024)S(1)} %copy-done.8, f32[1]{0:T(128)S(6)} %copy.13.dust_ref, f32[96,128,128]{2,1,0:T(8,128)S(1)} %get-tuple-element.20.keep, f32[16,128,128]{2,1,0:T(8,128)S(1)} %get-tuple-element.21.top_ref, ...), custom_call_target="tpu_custom_call" | custom-call | tf_op jit(solution)/shard_map/pallas_call | solution.py:317
  120.4 8.1 %all_to_all.28.x_ref = f32[4,32,128]{2,1,0:T(8,128)S(1)} all-to-all(f32[4,32,128]{2,1,0:T(8,128)S(1)} %get-tuple-element.26), channel_id=1, replica_groups={{0,8,16,24},{32,40,48,56},{64,72,80,88},{96,104,112,120},{128,136,144,1..., dimensions={0} | all-to-all | bytes 131072 | tf_op jit(solution)/shard_map/all_to_all | solution.py:310
  128.6 3.1 %collective-permute-start.11 = (f32[4,32,128]{2,1,0:T(8,128)S(1)}, f32[4,32,128]{2,1,0:T(8,128)S(1)}, u32[]{:S(2)}, u32[]{:S(2)}) collective-permute-start(f32[4,32,128]{2,1,0:T(8,128)S(1)} %all_to_all.28.x_ref), channel_id=1, source_target_pairs={{0,1},{1,0},{2,3},{3,2},{4,5},{5,4},{6,7},{7,6},{8,9},{9,8},{10,11... | collective-permute-start | bytes 196616 | tf_op jit(solution)/shard_map/ppermute | solution.py:286
  131.7 0.9 collective-permute-done.11.y_ref
  132.5 3.9 %shard_map.125 = (f32[48,128]{1,0:T(8,128)S(1)}, f32[4,32,128]{2,1,0:T(8,128)S(1)}, f32[12,128,128]{2,1,0:T(8,128)S(1)}, f32[2,128]{1,0:T(2,128)}) custom-call(s32[16,128]{1,0:T(8,128)S(1)} %get-tuple-element.18.cov_ref, s32[1024]{0:T(1024)S(1)} %copy-done.8, f32[1]{0:T(128)S(6)} %copy.13.dust_ref, f32[96,128,128]{2,1,0:T(8,128)S(1)} %get-tuple-element.20.keep, ...), custom_call_target="tpu_custom_call" | custom-call | tf_op jit(solution)/shard_map/pallas_call | solution.py:317
  136.4 8.1 %all_to_all.29.x_ref = f32[4,32,128]{2,1,0:T(8,128)S(1)} all-to-all(f32[4,32,128]{2,1,0:T(8,128)S(1)} %get-tuple-element.29), channel_id=1, replica_groups={{0,8,16,24},{32,40,48,56},{64,72,80,88},{96,104,112,120},{128,136,144,1..., dimensions={0} | all-to-all | bytes 131072 | tf_op jit(solution)/shard_map/all_to_all | solution.py:310
  144.6 3.2 %collective-permute-start.12 = (f32[4,32,128]{2,1,0:T(8,128)S(1)}, f32[4,32,128]{2,1,0:T(8,128)S(1)}, u32[]{:S(2)}, u32[]{:S(2)}) collective-permute-start(f32[4,32,128]{2,1,0:T(8,128)S(1)} %all_to_all.29.x_ref), channel_id=1, source_target_pairs={{0,1},{1,0},{2,3},{3,2},{4,5},{5,4},{6,7},{7,6},{8,9},{9,8},{10,11... | collective-permute-start | bytes 196616 | tf_op jit(solution)/shard_map/ppermute | solution.py:286
  147.7 0.9 collective-permute-done.12.y_ref
  148.6 2.4 %shard_map.126 = (f32[2,6,128,128]{3,2,1,0:T(8,128)}, f32[2,128]{1,0:T(2,128)}) custom-call(s32[16,128]{1,0:T(8,128)S(1)} %get-tuple-element.18.cov_ref, s32[1024]{0:T(1024)S(1)} %copy-done.8, f32[1]{0:T(128)S(6)} %copy.13.dust_ref, f32[12,128,128]{2,1,0:T(8,128)S(1)} %get-tuple-element.27.base_ref, f32[48,128]{1,0:T(8,128)S(1)} %get-tuple-element.28.s_in, ...), custom_call_target="tpu_custom_call" | custom-call | tf_op jit(solution)/shard_map/pallas_call | solution.py:317
  (15 shorter events, 0.0 us)
Async XLA Ops:
  0.6 0.9 copy-start.1
  1.5 0.7 copy-start.9
  2.2 0.7 copy-start.11
  2.9 94.1 %copy-start.8 = (s32[1024]{0:T(1024)S(1)}, s32[1024]{0:T(1024)}, u32[]{:S(2)}) copy-start(s32[1024]{0:T(1024)} %kpt_ref.9) | copy-start | bytes 12292
  17.4 22.0 %collective-permute-start.3 = (bf16[4,272,256]{2,1,0:T(8,128)(2,1)S(1)}, bf16[4,272,256]{2,1,0:T(8,128)(2,1)S(1)}, u32[]{:S(2)}, u32[]{:S(2)}) collective-permute-start(bf16[4,272,256]{2,1,0:T(8,128)(2,1)S(1)} %all_to_all.25.own), channel_id=1, source_target_pairs={{8,0},{16,8},{24,16},{32,24},{40,32},{48,40},{56,48},{64,56},{72,6... | collective-permute-start | bytes 1671176 | tf_op jit(solution)/shard_map/ppermute | solution.py:292
  29.0 16.7 %collective-permute-start.1 = (bf16[4,272,256]{2,1,0:T(8,128)(2,1)S(1)}, bf16[4,272,256]{2,1,0:T(8,128)(2,1)S(1)}, u32[]{:S(2)}, u32[]{:S(2)}) collective-permute-start(bf16[4,272,256]{2,1,0:T(8,128)(2,1)S(1)} %all_to_all.25.own), channel_id=1, source_target_pairs={{0,8},{8,16},{16,24},{24,32},{32,40},{40,48},{48,56},{56,64},{64,7... | collective-permute-start | bytes 1671176 | tf_op jit(solution)/shard_map/ppermute | solution.py:292
  30.9 16.7 %collective-permute-start = (bf16[4,272,256]{2,1,0:T(8,128)(2,1)S(1)}, bf16[4,272,256]{2,1,0:T(8,128)(2,1)S(1)}, u32[]{:S(2)}, u32[]{:S(2)}) collective-permute-start(bf16[4,272,256]{2,1,0:T(8,128)(2,1)S(1)} %all_to_all.25.own), channel_id=1, source_target_pairs={{0,1},{1,0},{2,3},{3,2},{4,5},{5,4},{6,7},{7,6},{8,9},{9,8},{10,11... | collective-permute-start | bytes 1671176 | tf_op jit(solution)/shard_map/ppermute | solution.py:286
  39.4 8.2 %collective-permute-start.4 = (bf16[4,272,256]{2,1,0:T(8,128)(2,1)S(1)}, bf16[4,272,256]{2,1,0:T(8,128)(2,1)S(1)}, u32[]{:S(2)}, u32[]{:S(2)}) collective-permute-start(bf16[4,272,256]{2,1,0:T(8,128)(2,1)S(1)} %collective-permute-done.3.high), channel_id=1, source_target_pairs={{0,1},{1,0},{2,3},{3,2},{4,5},{5,4},{6,7},{7,6},{8,9},{9,8},{10,11... | collective-permute-start | bytes 1671176 | tf_op jit(solution)/shard_map/ppermute | solution.py:286
  45.6 3.8 %collective-permute-start.2 = (bf16[4,272,256]{2,1,0:T(8,128)(2,1)S(1)}, bf16[4,272,256]{2,1,0:T(8,128)(2,1)S(1)}, u32[]{:S(2)}, u32[]{:S(2)}) collective-permute-start(bf16[4,272,256]{2,1,0:T(8,128)(2,1)S(1)} %collective-permute-done.1.low), channel_id=1, source_target_pairs={{0,1},{1,0},{2,3},{3,2},{4,5},{5,4},{6,7},{7,6},{8,9},{9,8},{10,11... | collective-permute-start | bytes 1671176 | tf_op jit(solution)/shard_map/ppermute | solution.py:286
  49.5 1.0 copy-start
  50.5 0.9 copy-start.2
  51.4 0.9 copy-start.3
  52.4 0.9 copy-start.4
  53.3 0.9 copy-start.5
  54.2 0.9 copy-start.6
  55.1 0.7 copy-start.7
  55.8 0.7 copy-start.10
  56.5 0.7 copy-start.12
  73.8 15.0 %collective-permute-start.8 = (bf16[4,256,256]{2,1,0:T(8,128)(2,1)S(1)}, bf16[4,256,256]{2,1,0:T(8,128)(2,1)S(1)}, u32[]{:S(2)}, u32[]{:S(2)}) collective-permute-start(bf16[4,256,256]{2,1,0:T(8,128)(2,1)S(1)} %all_to_all.26.own), channel_id=1, source_target_pairs={{8,0},{16,8},{24,16},{32,24},{40,32},{48,40},{56,48},{64,56},{72,6... | collective-permute-start | bytes 1572872 | tf_op jit(solution)/shard_map/ppermute | solution.py:292
  76.4 16.8 %collective-permute-start.6 = (bf16[4,256,256]{2,1,0:T(8,128)(2,1)S(1)}, bf16[4,256,256]{2,1,0:T(8,128)(2,1)S(1)}, u32[]{:S(2)}, u32[]{:S(2)}) collective-permute-start(bf16[4,256,256]{2,1,0:T(8,128)(2,1)S(1)} %all_to_all.26.own), channel_id=1, source_target_pairs={{0,8},{8,16},{16,24},{24,32},{32,40},{40,48},{48,56},{56,64},{64,7... | collective-permute-start | bytes 1572872 | tf_op jit(solution)/shard_map/ppermute | solution.py:292
  79.7 16.1 %collective-permute-start.5 = (bf16[4,256,256]{2,1,0:T(8,128)(2,1)S(1)}, bf16[4,256,256]{2,1,0:T(8,128)(2,1)S(1)}, u32[]{:S(2)}, u32[]{:S(2)}) collective-permute-start(bf16[4,256,256]{2,1,0:T(8,128)(2,1)S(1)} %all_to_all.26.own), channel_id=1, source_target_pairs={{0,1},{1,0},{2,3},{3,2},{4,5},{5,4},{6,7},{7,6},{8,9},{9,8},{10,11... | collective-permute-start | bytes 1572872 | tf_op jit(solution)/shard_map/ppermute | solution.py:286
  88.8 7.0 %collective-permute-start.9 = (bf16[4,256,256]{2,1,0:T(8,128)(2,1)S(1)}, bf16[4,256,256]{2,1,0:T(8,128)(2,1)S(1)}, u32[]{:S(2)}, u32[]{:S(2)}) collective-permute-start(bf16[4,256,256]{2,1,0:T(8,128)(2,1)S(1)} %collective-permute-done.8.high), channel_id=1, source_target_pairs={{0,1},{1,0},{2,3},{3,2},{4,5},{5,4},{6,7},{7,6},{8,9},{9,8},{10,11... | collective-permute-start | bytes 1572872 | tf_op jit(solution)/shard_map/ppermute | solution.py:286
  93.2 3.8 %collective-permute-start.7 = (bf16[4,256,256]{2,1,0:T(8,128)(2,1)S(1)}, bf16[4,256,256]{2,1,0:T(8,128)(2,1)S(1)}, u32[]{:S(2)}, u32[]{:S(2)}) collective-permute-start(bf16[4,256,256]{2,1,0:T(8,128)(2,1)S(1)} %collective-permute-done.6.low), channel_id=1, source_target_pairs={{0,1},{1,0},{2,3},{3,2},{4,5},{5,4},{6,7},{7,6},{8,9},{9,8},{10,11... | collective-permute-start | bytes 1572872 | tf_op jit(solution)/shard_map/ppermute | solution.py:286
  114.2 3.1 %collective-permute-start.10 = (f32[4,32,128]{2,1,0:T(8,128)S(1)}, f32[4,32,128]{2,1,0:T(8,128)S(1)}, u32[]{:S(2)}, u32[]{:S(2)}) collective-permute-start(f32[4,32,128]{2,1,0:T(8,128)S(1)} %all_to_all.27.x_ref), channel_id=1, source_target_pairs={{0,1},{1,0},{2,3},{3,2},{4,5},{5,4},{6,7},{7,6},{8,9},{9,8},{10,11... | collective-permute-start | bytes 196616 | tf_op jit(solution)/shard_map/ppermute | solution.py:286
  128.6 4.0 %collective-permute-start.11 = (f32[4,32,128]{2,1,0:T(8,128)S(1)}, f32[4,32,128]{2,1,0:T(8,128)S(1)}, u32[]{:S(2)}, u32[]{:S(2)}) collective-permute-start(f32[4,32,128]{2,1,0:T(8,128)S(1)} %all_to_all.28.x_ref), channel_id=1, source_target_pairs={{0,1},{1,0},{2,3},{3,2},{4,5},{5,4},{6,7},{7,6},{8,9},{9,8},{10,11... | collective-permute-start | bytes 196616 | tf_op jit(solution)/shard_map/ppermute | solution.py:286
  144.6 4.0 %collective-permute-start.12 = (f32[4,32,128]{2,1,0:T(8,128)S(1)}, f32[4,32,128]{2,1,0:T(8,128)S(1)}, u32[]{:S(2)}, u32[]{:S(2)}) collective-permute-start(f32[4,32,128]{2,1,0:T(8,128)S(1)} %all_to_all.29.x_ref), channel_id=1, source_target_pairs={{0,1},{1,0},{2,3},{3,2},{4,5},{5,4},{6,7},{7,6},{8,9},{9,8},{10,11... | collective-permute-start | bytes 196616 | tf_op jit(solution)/shard_map/ppermute | solution.py:286
